TPU v7x, 128 devices: a whole 4x4x4 slice. The times are simulated.
128 devices in a mesh: ctx: 16 (over y, z_lo, core), fsdp: 8 (over x, z_hi).
Axes of the slice: x: 4, y: 4, z: 4 (z_hi: 2, z_lo: 2; z = z_hi * 2 + z_lo), core: 2. Of those that a mesh axis runs over, the one named last changes fastest.
Arguments:
- layer_input: bfloat16 [8, 2048, 1024], P('fsdp', 'ctx'), may hold values from -6 to 6
- segment_ids: int32 [8, 2048], P('fsdp', 'ctx'), may hold values from 0 to 2, as said below
- norm_gain: bfloat16 [1024], P('fsdp'), may hold values from 0.5 to 1.5
- w_query: bfloat16 [1024, 512], P('fsdp'), may hold values from -0.1875 to 0.1875
- w_key: bfloat16 [1024, 128], P('fsdp'), may hold values from -0.1875 to 0.1875
- w_value: bfloat16 [1024, 128], P('fsdp'), may hold values from -0.1875 to 0.1875
- w_attn_out: bfloat16 [512, 1024], P('fsdp'), may hold values from -0.75 to 0.75
- w_gate_z: bfloat16 [1024, 1536], P('fsdp'), may hold values from -0.1875 to 0.1875
- w_inner: bfloat16 [1024, 1792], P('fsdp'), may hold values from -0.1875 to 0.1875
- w_step: bfloat16 [1024, 24], P('fsdp'), may hold values from -0.1875 to 0.1875
- conv_weight: bfloat16 [4, 1792], P(None, 'fsdp'), may hold values from -3 to 3
- conv_bias: bfloat16 [1792], P('fsdp'), may hold values from -3 to 3
- step_bias: bfloat16 [24], P('fsdp'), may hold values from -6 to -2
- decay_log: bfloat16 [24], P('fsdp'), may hold values from -4 to 1
- skip_gain: bfloat16 [24], P('fsdp'), may hold values from 0.5 to 1.5
- mixer_gain: bfloat16 [1536], P('fsdp'), may hold values from 0.5 to 1.5
- w_mixer_out: bfloat16 [1536, 1024], P('fsdp'), may hold values from -0.3125 to 0.3125
- ffn_gain: bfloat16 [1024], P('fsdp'), may hold values from 0.5 to 1.5
- w_gate: bfloat16 [1024, 2048], P('fsdp'), may hold values from -0.1875 to 0.1875
- w_up: bfloat16 [1024, 2048], P('fsdp'), may hold values from -0.1875 to 0.1875
- w_down: bfloat16 [2048, 1024], P('fsdp'), may hold values from -0.125 to 0.125
- out_grad: bfloat16 [8, 2048, 1024], P('fsdp', 'ctx'), may hold values from -6 to 6
Outputs:
- layer_output: bfloat16 [8, 2048, 1024], P('fsdp', 'ctx')
- input_grad: float32 [8, 2048, 1024], P('fsdp', 'ctx')
- grad_norm_gain: float32 [1024], P('fsdp')
- grad_w_query: float32 [1024, 512], P('fsdp')
- grad_w_key: float32 [1024, 128], P('fsdp')
- grad_w_value: float32 [1024, 128], P('fsdp')
- grad_w_attn_out: float32 [512, 1024], P('fsdp')
- grad_w_gate_z: float32 [1024, 1536], P('fsdp')
- grad_w_inner: float32 [1024, 1792], P('fsdp')
- grad_w_step: float32 [1024, 24], P('fsdp')
- grad_conv_weight: float32 [4, 1792], P(None, 'fsdp')
- grad_conv_bias: float32 [1792], P('fsdp')
- grad_step_bias: float32 [24], P('fsdp')
- grad_decay_log: float32 [24], P('fsdp')
- grad_skip_gain: float32 [24], P('fsdp')
- grad_mixer_gain: float32 [1536], P('fsdp')
- grad_w_mixer_out: float32 [1536, 1024], P('fsdp')
- grad_ffn_gain: float32 [1024], P('fsdp')
- grad_w_gate: float32 [1024, 2048], P('fsdp')
- grad_w_up: float32 [1024, 2048], P('fsdp')
- grad_w_down: float32 [2048, 1024], P('fsdp')
Inputs may be any that keep to these rules, and one draw needn't show every extreme that they name: `segment_ids`: each row holds three documents numbered 0, 1, 2 in order: document 0 ends within the first 128 positions and document 2 begins within the last 128.
All inputs are finite; a program needn't handle non-finite values.
Results may differ from a plain program's by a relative error of at most 0.025.
Values may be sent and summed in bfloat16 or wider, within the bound.
A program may use at most 192 MiB of HBM per device.

v0:
```python
import jax
import jax.numpy as jnp
from jax import lax
from jax.sharding import PartitionSpec as P

HEADS = 8
KV_HEADS = 2
HEAD_DIM = 64
SSM_HEADS = 24
SSM_DIM = 64
STATE = 128
CONV = 4


epsilon = 1e-05
rope_base = 10000.0
key_scale = 0.5
attn_out_scale = 0.8
mixer_out_scale = 0.5
gate_scale = 0.75
down_scale = 0.8
masked_score = -1e30
highest = lax.Precision.HIGHEST


def shifted(value, axis, steps):
    count = lax.axis_size(axis)
    first, last = (max(0, -steps), min(count, count - steps))
    return lax.ppermute(value, axis, [(source, source + steps) for source in range(first, last)])


def entering_2(part, axis, combine, identity):
    place = lax.axis_index(axis)
    gathered = jax.tree.map(lambda a: lax.all_gather(a, axis), part)
    state = jax.tree.map(lambda a, e: jnp.zeros_like(a) + jnp.asarray(e, a.dtype), part, identity)

    def one(turn, state):
        return combine(
            state, jax.tree.map(lambda a: lax.dynamic_index_in_dim(a, turn, 0, False), gathered)
        )

    return lax.fori_loop(0, place, one, state)


def carried_in(value, axis, combine, identity):
    peers, index = (lax.axis_size(axis), lax.axis_index(axis))
    everything = jax.tree.map(
        lambda part, kind: lax.all_gather(part.astype(kind), axis),
        value,
        jax.tree.map(lambda a: jnp.bfloat16 if a.dtype == jnp.float32 else a.dtype, value),
    )
    start = jax.tree.map(
        lambda part, zero: jnp.broadcast_to(jnp.asarray(zero, part.dtype), part.shape),
        value,
        identity,
    )

    def turn(k, before):
        at = peers - 1 - k
        reached = at > index
        new = combine(
            before, jax.tree.map(lambda part, own: part[at].astype(own.dtype), everything, value)
        )
        return jax.tree.map(lambda a, b: jnp.where(reached, a, b), new, before)

    return lax.fori_loop(0, peers, turn, start)


def matmul_f32(left_side, right_side):
    return jnp.dot(left_side, right_side, preferred_element_type=jnp.float32)


def left_trans(left_side, right_side):
    return lax.dot_general(
        left_side, right_side, (((0,), (0,)), ((), ())), preferred_element_type=jnp.float32
    )


def right_trans(left_side, right_side):
    return lax.dot_general(
        left_side, right_side, (((1,), (1,)), ((), ())), preferred_element_type=jnp.float32
    )


def rms_scale(values, gain_vec):
    return (
        values * lax.rsqrt(jnp.mean(values * values, axis=-1, keepdims=True) + epsilon) * gain_vec
    )


def rope_tables(positions):
    half_dim = HEAD_DIM // 2
    inverse = rope_base ** (-jnp.arange(half_dim, dtype=jnp.float32) / half_dim)
    angles = positions.astype(jnp.float32)[:, None] * inverse[None, :]
    return (jnp.cos(angles)[:, None, :], jnp.sin(angles)[:, None, :])


def rotate(values, angle_cos, angle_sin):
    half_dim = values.shape[-1] // 2
    first_half = values[..., :half_dim]
    second_half = values[..., half_dim:]
    return jnp.concatenate(
        [
            first_half * angle_cos - second_half * angle_sin,
            second_half * angle_cos + first_half * angle_sin,
        ],
        axis=-1,
    )


def rotate_back(values, angle_cos, angle_sin):
    half_dim = values.shape[-1] // 2
    first_half = values[..., :half_dim]
    second_half = values[..., half_dim:]
    return jnp.concatenate(
        [
            first_half * angle_cos + second_half * angle_sin,
            second_half * angle_cos - first_half * angle_sin,
        ],
        axis=-1,
    )


def conv_mix(extended, seg_ext, seg_here, conv_weight, conv_bias):
    row_count = seg_here.shape[0]
    summed = jnp.broadcast_to(conv_bias[None, :], (row_count, conv_bias.shape[0]))
    for offset in range(conv_weight.shape[0]):
        same_doc = (seg_ext[offset : offset + row_count] == seg_here)[:, None]
        summed = summed + conv_weight[offset][None, :] * jnp.where(
            same_doc, extended[offset : offset + row_count], 0.0
        )
    return jax.nn.silu(summed)


def mixer_features(
    extended, seg_ext, seg_here, step_raw, conv_weight, conv_bias, step_bias, decay_log
):
    mixed_rows = conv_mix(extended, seg_ext, seg_here, conv_weight, conv_bias)
    row_count = seg_here.shape[0]
    width_inner = SSM_HEADS * SSM_DIM
    values_ssm = mixed_rows[:, :width_inner].reshape(row_count, SSM_HEADS, SSM_DIM)
    input_map = mixed_rows[:, width_inner : width_inner + STATE]
    output_map = mixed_rows[:, width_inner + STATE :]
    step_size = jax.nn.softplus(step_raw + step_bias[None, :])
    log_decay = -step_size * jnp.exp(decay_log)[None, :]
    return (values_ssm, input_map, output_map, step_size, log_decay)


def ssd_states(values_ssm, input_map, step_size, log_decay, seg_here, seg_before):
    cumulative = jnp.cumsum(log_decay, axis=0)
    last_seg = seg_here[-1]
    tail_weight = (
        jnp.where(
            (seg_here == last_seg)[:, None], jnp.exp(cumulative[-1][None, :] - cumulative), 0.0
        )
        * step_size
    )
    weighted = tail_weight[:, :, None] * values_ssm
    block_state = jnp.einsum("shp,sn->hpn", weighted, input_map, precision=highest)
    block_decay = jnp.exp(cumulative[-1]) * (last_seg == seg_before).astype(jnp.float32)
    return (block_decay, block_state)


def ssd_output(
    values_ssm,
    input_map,
    output_map,
    step_size,
    log_decay,
    seg_here,
    seg_before,
    skip_gain,
    carried,
):
    row_count = seg_here.shape[0]
    cumulative = jnp.cumsum(log_decay, axis=0)
    order_idx = jnp.arange(row_count, dtype=jnp.int32)
    causal_same = (seg_here[:, None] == seg_here[None, :]) & (
        order_idx[:, None] >= order_idx[None, :]
    )
    keep_mask = causal_same[:, :, None]
    spread = cumulative[:, None, :] - cumulative[None, :, :]
    decay_mat = jnp.where(keep_mask, jnp.exp(jnp.where(keep_mask, spread, 0.0)), 0.0)
    pairing = jnp.dot(output_map, input_map.T, precision=highest)
    mixing = decay_mat * pairing[:, :, None] * step_size[None, :, :]
    result = jnp.einsum("tsh,shp->thp", mixing, values_ssm, precision=highest)
    entering = jnp.exp(cumulative) * (seg_here == seg_before).astype(jnp.float32)[:, None]
    result = result + entering[:, :, None] * jnp.einsum(
        "tn,hpn->thp", output_map, carried, precision=highest
    )
    return (result + skip_gain[None, :, None] * values_ssm, entering)


def gate_norm(result, gate_z, mixer_gain):
    flat_rows = result.reshape(gate_z.shape) * jax.nn.silu(gate_z)
    return rms_scale(flat_rows, mixer_gain)


def chain_step(earlier_part, later_part):
    decay_first, state_first = earlier_part
    decay_second, state_second = later_part
    return (decay_first * decay_second, decay_second[:, None, None] * state_first + state_second)


def head_forward(query_head, key_head, value_head, visible):
    scores = jnp.einsum("tgd,jd->gtj", query_head, key_head, preferred_element_type=jnp.float32)
    scores = jnp.where(visible[None], scores, masked_score)
    row_max = jnp.max(scores, axis=-1, keepdims=True)
    exp_scores = jnp.exp(scores - row_max)
    row_sum = jnp.sum(exp_scores, axis=-1, keepdims=True)
    prob_low = (exp_scores / row_sum).astype(jnp.bfloat16)
    attended = jnp.einsum("gtj,jd->tgd", prob_low, value_head, preferred_element_type=jnp.float32)
    return (attended, (row_max + jnp.log(row_sum))[..., 0])


def head_backward(query_head, key_head, value_head, grad_head, log_total, visible):
    scores = jnp.einsum("tgd,jd->gtj", query_head, key_head, preferred_element_type=jnp.float32)
    scores = jnp.where(visible[None], scores, masked_score)
    prob_full = jnp.where(visible[None], jnp.exp(scores - log_total[..., None]), 0.0)
    prob_low = prob_full.astype(jnp.bfloat16)
    grad_probs = jnp.einsum(
        "tgd,jd->gtj", grad_head, value_head, preferred_element_type=jnp.float32
    )
    inner_sum = jnp.sum(prob_full * grad_probs, axis=-1, keepdims=True)
    grad_scores = (prob_full * (grad_probs - inner_sum)).astype(jnp.bfloat16)
    grad_query = jnp.einsum(
        "gtj,jd->tgd", grad_scores, key_head, preferred_element_type=jnp.float32
    )
    grad_key = jnp.einsum(
        "gtj,tgd->jd", grad_scores, query_head, preferred_element_type=jnp.float32
    )
    grad_value = jnp.einsum("gtj,tgd->jd", prob_low, grad_head, preferred_element_type=jnp.float32)
    return (grad_query, grad_key, grad_value)


def local(
    layer_input,
    segment_ids,
    norm_gain,
    w_query,
    w_key,
    w_value,
    w_attn_out,
    w_gate_z,
    w_inner,
    w_step,
    conv_weight,
    conv_bias,
    step_bias,
    decay_log,
    skip_gain,
    mixer_gain,
    w_mixer_out,
    ffn_gain,
    w_gate,
    w_up,
    w_down,
    out_grad,
):
    tok_rows = layer_input.shape[1]
    ctx_here = lax.axis_index("ctx")
    first_pos = ctx_here * tok_rows
    seg_all = lax.all_gather(segment_ids, "ctx", axis=1, tiled=True)[0]
    seg_here = segment_ids[0]
    seq_total = seg_all.shape[0]
    pos_here = first_pos + jnp.arange(tok_rows, dtype=jnp.int32)
    pos_all = jnp.arange(seq_total, dtype=jnp.int32)
    residual_in = layer_input[0].astype(jnp.float32)
    grad_final = out_grad[0].astype(jnp.float32)
    group_size = HEADS // KV_HEADS
    kv_width = KV_HEADS * HEAD_DIM
    gain_one, query_full, key_full, value_full, attn_out_full = (
        lax.all_gather(norm_gain, "fsdp", axis=0, tiled=True),
        lax.all_gather(w_query, "fsdp", axis=0, tiled=True),
        lax.all_gather(w_key, "fsdp", axis=0, tiled=True),
        lax.all_gather(w_value, "fsdp", axis=0, tiled=True),
        lax.all_gather(w_attn_out, "fsdp", axis=0, tiled=True),
    )
    gain_one_f = gain_one.astype(jnp.float32)
    normed_low = rms_scale(residual_in, gain_one_f).astype(jnp.bfloat16)
    angle_cos, angle_sin = rope_tables(pos_here)
    query_rot = rotate(
        matmul_f32(normed_low, query_full).reshape(tok_rows, HEADS, HEAD_DIM), angle_cos, angle_sin
    ) * HEAD_DIM ** (-0.5)
    key_rot = (
        rotate(
            matmul_f32(normed_low, key_full).reshape(tok_rows, KV_HEADS, HEAD_DIM),
            angle_cos,
            angle_sin,
        )
        * key_scale
    )
    value_proj = matmul_f32(normed_low, value_full)
    query_low = query_rot.astype(jnp.bfloat16)
    local_kv = jnp.concatenate(
        [key_rot.reshape(tok_rows, kv_width).astype(jnp.bfloat16), value_proj.astype(jnp.bfloat16)],
        axis=1,
    )
    kv_all = lax.all_gather(local_kv, "ctx", axis=0, tiled=True)
    key_heads = kv_all[:, :kv_width].reshape(seq_total, KV_HEADS, HEAD_DIM).transpose(1, 0, 2)
    value_heads = kv_all[:, kv_width:].reshape(seq_total, KV_HEADS, HEAD_DIM).transpose(1, 0, 2)
    query_heads = query_low.reshape(tok_rows, KV_HEADS, group_size, HEAD_DIM).transpose(1, 0, 2, 3)
    visible = (pos_all[None, :] <= pos_here[:, None]) & (seg_all[None, :] == seg_here[:, None])
    attended, log_total = lax.map(
        lambda head_parts: head_forward(head_parts[0], head_parts[1], head_parts[2], visible),
        (query_heads, key_heads, value_heads),
    )
    attn_low = (
        attended.transpose(1, 0, 2, 3).reshape(tok_rows, HEADS * HEAD_DIM).astype(jnp.bfloat16)
    )
    attn_branch = matmul_f32(attn_low, attn_out_full) * attn_out_scale
    (
        gate_z_full,
        inner_full,
        step_full,
        conv_full,
        conv_bias_full,
        step_bias_full,
        decay_full,
        skip_full,
        mixer_gain_full,
        mixer_out_full,
    ) = (
        lax.all_gather(w_gate_z, "fsdp", axis=0, tiled=True),
        lax.all_gather(w_inner, "fsdp", axis=0, tiled=True),
        lax.all_gather(w_step, "fsdp", axis=0, tiled=True),
        lax.all_gather(conv_weight, "fsdp", axis=1, tiled=True),
        lax.all_gather(conv_bias, "fsdp", axis=0, tiled=True),
        lax.all_gather(step_bias, "fsdp", axis=0, tiled=True),
        lax.all_gather(decay_log, "fsdp", axis=0, tiled=True),
        lax.all_gather(skip_gain, "fsdp", axis=0, tiled=True),
        lax.all_gather(mixer_gain, "fsdp", axis=0, tiled=True),
        lax.all_gather(w_mixer_out, "fsdp", axis=0, tiled=True),
    )
    conv_f = conv_full.astype(jnp.float32)
    conv_bias_f = conv_bias_full.astype(jnp.float32)
    step_bias_f = step_bias_full.astype(jnp.float32)
    decay_f = decay_full.astype(jnp.float32)
    skip_f = skip_full.astype(jnp.float32)
    mixer_gain_f = mixer_gain_full.astype(jnp.float32)
    gate_z = matmul_f32(normed_low, gate_z_full)
    inner_pre = matmul_f32(normed_low, inner_full)
    step_raw = matmul_f32(normed_low, step_full)
    rim_rows = CONV - 1
    rim_in = shifted(inner_pre[tok_rows - rim_rows :], "ctx", 1)
    extended = jnp.concatenate([rim_in, inner_pre], axis=0)
    rim_start = jnp.maximum(first_pos - rim_rows, 0)
    seg_rim = lax.dynamic_slice_in_dim(seg_all, rim_start, rim_rows)
    seg_ext = jnp.concatenate([seg_rim, seg_here])
    seg_prior = lax.dynamic_index_in_dim(seg_all, jnp.maximum(first_pos - 1, 0), keepdims=False)
    seg_before = jnp.where(ctx_here > 0, seg_prior, -1)
    values_ssm, input_map, output_map, step_size, log_decay = mixer_features(
        extended, seg_ext, seg_here, step_raw, conv_f, conv_bias_f, step_bias_f, decay_f
    )
    block_decay, block_state = ssd_states(
        values_ssm, input_map, step_size, log_decay, seg_here, seg_before
    )
    unit_decay = jnp.ones_like(block_decay)
    empty_state = jnp.zeros_like(block_state)
    _, carried = entering_2(
        (block_decay, block_state), "ctx", chain_step, (unit_decay, empty_state)
    )
    mixer_result, entering = ssd_output(
        values_ssm,
        input_map,
        output_map,
        step_size,
        log_decay,
        seg_here,
        seg_before,
        skip_f,
        carried,
    )
    mixer_low = gate_norm(mixer_result, gate_z, mixer_gain_f).astype(jnp.bfloat16)
    mixer_branch = matmul_f32(mixer_low, mixer_out_full) * mixer_out_scale
    middle = residual_in + attn_branch + mixer_branch
    gain_two, gate_full, up_full, down_full = (
        lax.all_gather(ffn_gain, "fsdp", axis=0, tiled=True),
        lax.all_gather(w_gate, "fsdp", axis=0, tiled=True),
        lax.all_gather(w_up, "fsdp", axis=0, tiled=True),
        lax.all_gather(w_down, "fsdp", axis=0, tiled=True),
    )
    gain_two_f = gain_two.astype(jnp.float32)
    normed_two_low = rms_scale(middle, gain_two_f).astype(jnp.bfloat16)
    gate_pre = matmul_f32(normed_two_low, gate_full) * gate_scale
    up_pre = matmul_f32(normed_two_low, up_full)
    hidden_low = (jax.nn.silu(gate_pre) * up_pre).astype(jnp.bfloat16)
    layer_out = middle + matmul_f32(hidden_low, down_full) * down_scale
    weights_back = (
        lax.all_gather(norm_gain, "fsdp", axis=0, tiled=True),
        lax.all_gather(w_query, "fsdp", axis=0, tiled=True),
        lax.all_gather(w_key, "fsdp", axis=0, tiled=True),
        lax.all_gather(w_value, "fsdp", axis=0, tiled=True),
        lax.all_gather(w_attn_out, "fsdp", axis=0, tiled=True),
        lax.all_gather(w_gate_z, "fsdp", axis=0, tiled=True),
        lax.all_gather(w_inner, "fsdp", axis=0, tiled=True),
        lax.all_gather(w_step, "fsdp", axis=0, tiled=True),
        lax.all_gather(w_mixer_out, "fsdp", axis=0, tiled=True),
        lax.all_gather(w_gate, "fsdp", axis=0, tiled=True),
        lax.all_gather(w_up, "fsdp", axis=0, tiled=True),
        lax.all_gather(w_down, "fsdp", axis=0, tiled=True),
    )
    (
        gain_one,
        query_full,
        key_full,
        value_full,
        attn_out_full,
        gate_z_full,
        inner_full,
        step_full,
        mixer_out_full,
        gate_full,
        up_full,
        down_full,
    ) = weights_back
    grad_down_in = (grad_final * down_scale).astype(jnp.bfloat16)
    grad_w_down = left_trans(hidden_low, grad_down_in)
    grad_hidden = right_trans(grad_down_in, down_full)
    gate_sig = jax.nn.sigmoid(gate_pre)
    grad_gate_in = (
        grad_hidden * up_pre * gate_sig * (1.0 + gate_pre * (1.0 - gate_sig)) * gate_scale
    ).astype(jnp.bfloat16)
    grad_up_in = (grad_hidden * gate_pre * gate_sig).astype(jnp.bfloat16)
    grad_w_gate = left_trans(normed_two_low, grad_gate_in)
    grad_w_up = left_trans(normed_two_low, grad_up_in)
    grad_normed_two = right_trans(grad_gate_in, gate_full) + right_trans(grad_up_in, up_full)
    _, pull_two = jax.vjp(rms_scale, middle, gain_two_f)
    grad_mid_norm, grad_gain_two = pull_two(grad_normed_two)
    grad_middle = grad_final + grad_mid_norm
    grad_mixer_in = (grad_middle * mixer_out_scale).astype(jnp.bfloat16)
    grad_w_mixer_out = left_trans(mixer_low, grad_mixer_in)
    grad_mixer_normed = right_trans(grad_mixer_in, mixer_out_full)
    _, pull_gate = jax.vjp(gate_norm, mixer_result, gate_z, mixer_gain_f)
    grad_result, grad_gate_z, grad_mixer_gain = pull_gate(grad_mixer_normed)
    grad_weighted = grad_result * entering[:, :, None]
    grad_carried = jnp.einsum("thp,tn->hpn", grad_weighted, output_map, precision=highest)
    _, grad_out_state = carried_in(
        (block_decay, grad_carried), "ctx", chain_step, (unit_decay, empty_state)
    )
    grad_block_decay = jnp.sum(grad_out_state * carried, axis=(1, 2))

    def mixer_core(
        core_ext,
        core_step,
        core_conv,
        core_conv_bias,
        core_step_bias,
        core_decay,
        core_skip,
        core_carried,
    ):
        core_values, core_input, core_output, core_size, core_log = mixer_features(
            core_ext,
            seg_ext,
            seg_here,
            core_step,
            core_conv,
            core_conv_bias,
            core_step_bias,
            core_decay,
        )
        core_block_decay, core_block_state = ssd_states(
            core_values, core_input, core_size, core_log, seg_here, seg_before
        )
        core_result, _ = ssd_output(
            core_values,
            core_input,
            core_output,
            core_size,
            core_log,
            seg_here,
            seg_before,
            core_skip,
            core_carried,
        )
        return (core_result, core_block_decay, core_block_state)

    _, pull_core = jax.vjp(
        mixer_core, extended, step_raw, conv_f, conv_bias_f, step_bias_f, decay_f, skip_f, carried
    )
    grad_ext, grad_step_raw, grad_conv, grad_conv_bias, grad_step_bias, grad_decay, grad_skip, _ = (
        pull_core((grad_result, grad_block_decay, grad_out_state))
    )
    rim_back = shifted(grad_ext[:rim_rows], "ctx", -1)
    grad_inner_pre = grad_ext[rim_rows:] + jnp.pad(rim_back, ((tok_rows - rim_rows, 0), (0, 0)))
    grad_inner_low = grad_inner_pre.astype(jnp.bfloat16)
    grad_gate_z_low = grad_gate_z.astype(jnp.bfloat16)
    grad_step_low = grad_step_raw.astype(jnp.bfloat16)
    grad_w_gate_z = left_trans(normed_low, grad_gate_z_low)
    grad_w_inner = left_trans(normed_low, grad_inner_low)
    grad_w_step = left_trans(normed_low, grad_step_low)
    grad_normed_one = (
        right_trans(grad_gate_z_low, gate_z_full)
        + right_trans(grad_inner_low, inner_full)
        + right_trans(grad_step_low, step_full)
    )
    grad_attn_in = (grad_middle * attn_out_scale).astype(jnp.bfloat16)
    grad_w_attn_out = left_trans(attn_low, grad_attn_in)
    grad_attended = right_trans(grad_attn_in, attn_out_full).astype(jnp.bfloat16)
    grad_heads = grad_attended.reshape(tok_rows, KV_HEADS, group_size, HEAD_DIM).transpose(
        1, 0, 2, 3
    )
    grad_query_h, grad_key_h, grad_value_h = lax.map(
        lambda head_parts: head_backward(
            head_parts[0], head_parts[1], head_parts[2], head_parts[3], head_parts[4], visible
        ),
        (query_heads, key_heads, value_heads, grad_heads, log_total),
    )
    grad_kv_terms = jnp.concatenate(
        [
            grad_key_h.transpose(1, 0, 2).reshape(seq_total, kv_width),
            grad_value_h.transpose(1, 0, 2).reshape(seq_total, kv_width),
        ],
        axis=1,
    )
    grad_kv = lax.psum_scatter(
        grad_kv_terms.astype(jnp.bfloat16), "ctx", scatter_dimension=0, tiled=True
    ).astype(jnp.float32)
    grad_key_rot = grad_kv[:, :kv_width].reshape(tok_rows, KV_HEADS, HEAD_DIM)
    grad_value_low = grad_kv[:, kv_width:].astype(jnp.bfloat16)
    grad_key_low = (
        (rotate_back(grad_key_rot, angle_cos, angle_sin) * key_scale)
        .reshape(tok_rows, kv_width)
        .astype(jnp.bfloat16)
    )
    grad_query = grad_query_h.transpose(1, 0, 2, 3).reshape(tok_rows, HEADS, HEAD_DIM)
    grad_query_low = (
        (rotate_back(grad_query, angle_cos, angle_sin) * HEAD_DIM ** (-0.5))
        .reshape(tok_rows, HEADS * HEAD_DIM)
        .astype(jnp.bfloat16)
    )
    grad_w_query = left_trans(normed_low, grad_query_low)
    grad_w_key = left_trans(normed_low, grad_key_low)
    grad_w_value = left_trans(normed_low, grad_value_low)
    grad_normed_one = (
        grad_normed_one
        + right_trans(grad_query_low, query_full)
        + right_trans(grad_key_low, key_full)
        + right_trans(grad_value_low, value_full)
    )
    _, pull_one = jax.vjp(rms_scale, residual_in, gain_one.astype(jnp.float32))
    grad_in_norm, grad_gain_one = pull_one(grad_normed_one)
    input_grad = grad_middle + grad_in_norm
    (
        shard_gain_one,
        shard_query,
        shard_key,
        shard_value,
        shard_attn_out,
        shard_gate_z,
        shard_inner,
        shard_step,
        shard_conv,
        shard_conv_bias,
        shard_step_bias,
        shard_decay,
        shard_skip,
        shard_mixer_gain,
        shard_mixer_out,
        shard_gain_two,
        shard_gate,
        shard_up,
        shard_down,
    ) = (
        lax.psum_scatter(
            grad_gain_one.astype(jnp.bfloat16), "fsdp", scatter_dimension=0, tiled=True
        ).astype(jnp.float32),
        lax.psum_scatter(
            grad_w_query.astype(jnp.bfloat16), "fsdp", scatter_dimension=0, tiled=True
        ).astype(jnp.float32),
        lax.psum_scatter(
            grad_w_key.astype(jnp.bfloat16), "fsdp", scatter_dimension=0, tiled=True
        ).astype(jnp.float32),
        lax.psum_scatter(
            grad_w_value.astype(jnp.bfloat16), "fsdp", scatter_dimension=0, tiled=True
        ).astype(jnp.float32),
        lax.psum_scatter(
            grad_w_attn_out.astype(jnp.bfloat16), "fsdp", scatter_dimension=0, tiled=True
        ).astype(jnp.float32),
        lax.psum_scatter(
            grad_w_gate_z.astype(jnp.bfloat16), "fsdp", scatter_dimension=0, tiled=True
        ).astype(jnp.float32),
        lax.psum_scatter(
            grad_w_inner.astype(jnp.bfloat16), "fsdp", scatter_dimension=0, tiled=True
        ).astype(jnp.float32),
        lax.psum_scatter(
            grad_w_step.astype(jnp.bfloat16), "fsdp", scatter_dimension=0, tiled=True
        ).astype(jnp.float32),
        lax.psum_scatter(
            grad_conv.astype(jnp.bfloat16), "fsdp", scatter_dimension=1, tiled=True
        ).astype(jnp.float32),
        lax.psum_scatter(
            grad_conv_bias.astype(jnp.bfloat16), "fsdp", scatter_dimension=0, tiled=True
        ).astype(jnp.float32),
        lax.psum_scatter(
            grad_step_bias.astype(jnp.bfloat16), "fsdp", scatter_dimension=0, tiled=True
        ).astype(jnp.float32),
        lax.psum_scatter(
            grad_decay.astype(jnp.bfloat16), "fsdp", scatter_dimension=0, tiled=True
        ).astype(jnp.float32),
        lax.psum_scatter(
            grad_skip.astype(jnp.bfloat16), "fsdp", scatter_dimension=0, tiled=True
        ).astype(jnp.float32),
        lax.psum_scatter(
            grad_mixer_gain.astype(jnp.bfloat16), "fsdp", scatter_dimension=0, tiled=True
        ).astype(jnp.float32),
        lax.psum_scatter(
            grad_w_mixer_out.astype(jnp.bfloat16), "fsdp", scatter_dimension=0, tiled=True
        ).astype(jnp.float32),
        lax.psum_scatter(
            grad_gain_two.astype(jnp.bfloat16), "fsdp", scatter_dimension=0, tiled=True
        ).astype(jnp.float32),
        lax.psum_scatter(
            grad_w_gate.astype(jnp.bfloat16), "fsdp", scatter_dimension=0, tiled=True
        ).astype(jnp.float32),
        lax.psum_scatter(
            grad_w_up.astype(jnp.bfloat16), "fsdp", scatter_dimension=0, tiled=True
        ).astype(jnp.float32),
        lax.psum_scatter(
            grad_w_down.astype(jnp.bfloat16), "fsdp", scatter_dimension=0, tiled=True
        ).astype(jnp.float32),
    )
    totals = (
        lax.psum(shard_gain_one.astype(jnp.bfloat16), "ctx").astype(jnp.float32),
        lax.psum(shard_query.astype(jnp.bfloat16), "ctx").astype(jnp.float32),
        lax.psum(shard_key.astype(jnp.bfloat16), "ctx").astype(jnp.float32),
        lax.psum(shard_value.astype(jnp.bfloat16), "ctx").astype(jnp.float32),
        lax.psum(shard_attn_out.astype(jnp.bfloat16), "ctx").astype(jnp.float32),
        lax.psum(shard_gate_z.astype(jnp.bfloat16), "ctx").astype(jnp.float32),
        lax.psum(shard_inner.astype(jnp.bfloat16), "ctx").astype(jnp.float32),
        lax.psum(shard_step.astype(jnp.bfloat16), "ctx").astype(jnp.float32),
        lax.psum(shard_conv.astype(jnp.bfloat16), "ctx").astype(jnp.float32),
        lax.psum(shard_conv_bias.astype(jnp.bfloat16), "ctx").astype(jnp.float32),
        lax.psum(shard_step_bias.astype(jnp.bfloat16), "ctx").astype(jnp.float32),
        lax.psum(shard_decay.astype(jnp.bfloat16), "ctx").astype(jnp.float32),
        lax.psum(shard_skip.astype(jnp.bfloat16), "ctx").astype(jnp.float32),
        lax.psum(shard_mixer_gain.astype(jnp.bfloat16), "ctx").astype(jnp.float32),
        lax.psum(shard_mixer_out.astype(jnp.bfloat16), "ctx").astype(jnp.float32),
        lax.psum(shard_gain_two.astype(jnp.bfloat16), "ctx").astype(jnp.float32),
        lax.psum(shard_gate.astype(jnp.bfloat16), "ctx").astype(jnp.float32),
        lax.psum(shard_up.astype(jnp.bfloat16), "ctx").astype(jnp.float32),
        lax.psum(shard_down.astype(jnp.bfloat16), "ctx").astype(jnp.float32),
    )
    return (
        layer_out.astype(jnp.bfloat16)[None],
        input_grad[None],
        totals[0],
        totals[1],
        totals[2],
        totals[3],
        totals[4],
        totals[5],
        totals[6],
        totals[7],
        totals[8],
        totals[9],
        totals[10],
        totals[11],
        totals[12],
        totals[13],
        totals[14],
        totals[15],
        totals[16],
        totals[17],
        totals[18],
    )


def solution(mesh):
    in_specs = (
        P("fsdp", "ctx", None),
        P("fsdp", "ctx"),
        P("fsdp"),
        P("fsdp", None),
        P("fsdp", None),
        P("fsdp", None),
        P("fsdp", None),
        P("fsdp", None),
        P("fsdp", None),
        P("fsdp", None),
        P(None, "fsdp"),
        P("fsdp"),
        P("fsdp"),
        P("fsdp"),
        P("fsdp"),
        P("fsdp"),
        P("fsdp", None),
        P("fsdp"),
        P("fsdp", None),
        P("fsdp", None),
        P("fsdp", None),
        P("fsdp", "ctx", None),
    )
    out_specs = (
        P("fsdp", "ctx", None),
        P("fsdp", "ctx", None),
        P("fsdp"),
        P("fsdp", None),
        P("fsdp", None),
        P("fsdp", None),
        P("fsdp", None),
        P("fsdp", None),
        P("fsdp", None),
        P("fsdp", None),
        P(None, "fsdp"),
        P("fsdp"),
        P("fsdp"),
        P("fsdp"),
        P("fsdp"),
        P("fsdp"),
        P("fsdp", None),
        P("fsdp"),
        P("fsdp", None),
        P("fsdp", None),
        P("fsdp", None),
    )
    return jax.shard_map(local, mesh=mesh, in_specs=in_specs, out_specs=out_specs, check_vma=False)
```

profile of v0, /device:TPU:1, one launch (start us, length us, event | category | flops | bytes accessed | tf_op | source)
XLA Modules:
  0.0 2032.3 jit_solution(15691449159399494032)
XLA Ops:
  30.1 28.9 %all_gather.96 = bf16[1024,128]{1,0:T(8,128)(2,1)S(1)} all-gather(bf16[128,128]{1,0:T(8,128)(2,1)} %param.34), channel_id=1, replica_groups=mesh['ctx'=16,'fsdp'=8] {'fsdp'}, dimensions={0}, use_global_device_ids=true | all-gather | bytes 294912 | tf_op jit(solution)/shard_map/all_gather | solution.py:275
  61.9 29.3 %all_gather.97 = bf16[1024,128]{1,0:T(8,128)(2,1)S(1)} all-gather(bf16[128,128]{1,0:T(8,128)(2,1)} %param.35), channel_id=1, replica_groups=mesh['ctx'=16,'fsdp'=8] {'fsdp'}, dimensions={0}, use_global_device_ids=true | all-gather | bytes 294912 | tf_op jit(solution)/shard_map/all_gather | solution.py:276
  114.4 25.5 %all_gather.105 = bf16[1024,24]{0,1:T(8,128)(2,1)S(1)} all-gather(bf16[128,24]{0,1:T(8,128)(2,1)S(1)} %copy-done.127), channel_id=1, replica_groups=mesh['ctx'=16,'fsdp'=8] {'fsdp'}, dimensions={0}, use_global_device_ids=true | all-gather | bytes 55296 | tf_op jit(solution)/shard_map/all_gather | solution.py:326
  140.0 43.2 %all_gather.99 = s32[1,2048]{1,0:T(1,128)S(1)} all-gather(s32[1,128]{1,0:T(1,128)S(1)} %copy-done.71), channel_id=1, replica_groups=mesh['ctx'=16,'fsdp'=8] {'ctx'}, dimensions={1}, use_global_device_ids=true | all-gather | bytes 8704 | tf_op jit(solution)/shard_map/all_gather | solution.py:263
  303.8 57.9 %all-gather.27.cloned.1.call-done = bf16[1024,1536]{1,0:T(8,128)(2,1)} async-done(((bf16[128,1536]{1,0:T(8,128)(2,1)}), bf16[1024,1536]{1,0:T(8,128)(2,1)}) %all-gather.27.cloned.1.call-update) | async-done | bytes 3145744 | tf_op jit(solution)/shard_map/all_gather | solution.py:324
  365.3 60.2 %all-gather.29.cloned.1.call-done = bf16[1536,1024]{1,0:T(8,128)(2,1)} async-done(((bf16[192,1024]{1,0:T(8,128)(2,1)}), bf16[1536,1024]{1,0:T(8,128)(2,1)}) %all-gather.29.cloned.1.call-update) | async-done | bytes 3145744 | tf_op jit(solution)/shard_map/all_gather | solution.py:333
  428.4 69.3 %all-gather.31.cloned.1.call-done = bf16[1024,2048]{1,0:T(8,128)(2,1)} async-done(((bf16[128,2048]{1,0:T(8,128)(2,1)}), bf16[1024,2048]{1,0:T(8,128)(2,1)}) %all-gather.31.cloned.1.call-update) | async-done | bytes 4194320 | tf_op jit(solution)/shard_map/all_gather | solution.py:379
  501.6 67.8 %all-gather.33.cloned.1.call-done = bf16[1024,2048]{1,0:T(8,128)(2,1)} async-done(((bf16[128,2048]{1,0:T(8,128)(2,1)}), bf16[1024,2048]{1,0:T(8,128)(2,1)}) %all-gather.33.cloned.1.call-update) | async-done | bytes 4194320 | tf_op jit(solution)/shard_map/all_gather | solution.py:380
  573.3 67.6 %all-gather.35.cloned.1.call-done = bf16[2048,1024]{1,0:T(8,128)(2,1)} async-done(((bf16[256,1024]{1,0:T(8,128)(2,1)}), bf16[2048,1024]{1,0:T(8,128)(2,1)}) %all-gather.35.cloned.1.call-update) | async-done | bytes 4194320 | tf_op jit(solution)/shard_map/all_gather | solution.py:381
  732.8 46.6 %all-gather.39.cloned.1.call-done = bf16[384,64,128]{2,1,0:T(8,128)(2,1)} async-done(((bf16[24,64,128]{2,1,0:T(8,128)(2,1)}), bf16[384,64,128]{2,1,0:T(8,128)(2,1)}) %all-gather.39.cloned.1.call-update) | async-done | bytes 6291472 | tf_op jit(solution)/shard_map/all_gather | solution.py:48
  866.5 34.0 %all-reduce.28 = (bf16[1024]{0:T(1024)(128)(2,1)S(1)}, bf16[1792]{0:T(1024)(128)(2,1)S(1)}, bf16[24]{0:T(256)(128)(2,1)S(1)}, bf16[24]{0:T(256)(128)(2,1)S(1)}, ...) all-reduce(bf16[1024]{0:T(1024)(128)(2,1)S(1)} %get-tuple-element.3, ...), channel_id=5, replica_groups=mesh['ctx'=16,'fsdp'=8] {'fsdp'}, use_global_device_ids=true, to_apply=%region_30.31.clone | all-reduce | flops 5448 | bytes 21792
  906.0 52.0 %reduce-scatter.42.cloned.1.call-done = bf16[128,24]{1,0:T(8,128)(2,1)} async-done(((bf16[1024,24]{1,0:T(8,128)(2,1)}), bf16[128,24]{1,0:T(8,128)(2,1)}) %reduce-scatter.42.cloned.1.call-update) | async-done | bytes 6160
  959.5 72.1 %reduce-scatter.22.cloned.1.call-done = bf16[128,128]{1,0:T(8,128)(2,1)} async-done(((bf16[1024,128]{1,0:T(8,128)(2,1)}), bf16[128,128]{1,0:T(8,128)(2,1)}) %reduce-scatter.22.cloned.1.call-update) | async-done | bytes 32784 | tf_op jit(solution)/shard_map/reduce_scatter | solution.py:572
  1031.6 73.1 %reduce-scatter.24.cloned.1.call-done = bf16[128,128]{1,0:T(8,128)(2,1)} async-done(((bf16[1024,128]{1,0:T(8,128)(2,1)}), bf16[128,128]{1,0:T(8,128)(2,1)}) %reduce-scatter.24.cloned.1.call-update) | async-done | bytes 32784 | tf_op jit(solution)/shard_map/reduce_scatter | solution.py:575
  1104.8 75.5 %reduce-scatter.20.cloned.1.call-done = bf16[128,512]{1,0:T(8,128)(2,1)} async-done(((bf16[1024,512]{1,0:T(8,128)(2,1)}), bf16[128,512]{1,0:T(8,128)(2,1)}) %reduce-scatter.20.cloned.1.call-update) | async-done | bytes 131088 | tf_op jit(solution)/shard_map/reduce_scatter | solution.py:569
  1180.3 75.1 %reduce-scatter.26.cloned.1.call-done = bf16[64,1024]{1,0:T(8,128)(2,1)} async-done(((bf16[512,1024]{1,0:T(8,128)(2,1)}), bf16[64,1024]{1,0:T(8,128)(2,1)}) %reduce-scatter.26.cloned.1.call-update) | async-done | bytes 131088 | tf_op jit(solution)/shard_map/reduce_scatter | solution.py:578
  1255.4 83.8 %reduce-scatter.32.cloned.1.call-done = bf16[192,1024]{1,0:T(8,128)(2,1)} async-done(((bf16[1536,1024]{1,0:T(8,128)(2,1)}), bf16[192,1024]{1,0:T(8,128)(2,1)}) %reduce-scatter.32.cloned.1.call-update) | async-done | bytes 393232 | tf_op jit(solution)/shard_map/reduce_scatter | solution.py:608
  1339.2 82.3 %reduce-scatter.28.cloned.1.call-done = bf16[128,1536]{1,0:T(8,128)(2,1)} async-done(((bf16[1024,1536]{1,0:T(8,128)(2,1)}), bf16[128,1536]{1,0:T(8,128)(2,1)}) %reduce-scatter.28.cloned.1.call-update) | async-done | bytes 393232 | tf_op jit(solution)/shard_map/reduce_scatter | solution.py:581
  1421.5 88.0 %reduce-scatter.34.cloned.1.call-done = bf16[128,2048]{1,0:T(8,128)(2,1)} async-done(((bf16[1024,2048]{1,0:T(8,128)(2,1)}), bf16[128,2048]{1,0:T(8,128)(2,1)}) %reduce-scatter.34.cloned.1.call-update) | async-done | bytes 524304 | tf_op jit(solution)/shard_map/reduce_scatter | solution.py:614
  1509.5 87.9 %reduce-scatter.36.cloned.1.call-done = bf16[128,2048]{1,0:T(8,128)(2,1)} async-done(((bf16[1024,2048]{1,0:T(8,128)(2,1)}), bf16[128,2048]{1,0:T(8,128)(2,1)}) %reduce-scatter.36.cloned.1.call-update) | async-done | bytes 524304 | tf_op jit(solution)/shard_map/reduce_scatter | solution.py:617
  1597.4 88.0 %reduce-scatter.38.cloned.1.call-done = bf16[256,1024]{1,0:T(8,128)(2,1)} async-done(((bf16[2048,1024]{1,0:T(8,128)(2,1)}), bf16[256,1024]{1,0:T(8,128)(2,1)}) %reduce-scatter.38.cloned.1.call-update) | async-done | bytes 524304 | tf_op jit(solution)/shard_map/reduce_scatter | solution.py:620
  1685.4 85.4 %reduce-scatter.30.cloned.1.call-done = bf16[128,1792]{1,0:T(8,128)(2,1)} async-done(((bf16[1024,1792]{1,0:T(8,128)(2,1)}), bf16[128,1792]{1,0:T(8,128)(2,1)}) %reduce-scatter.30.cloned.1.call-update) | async-done | bytes 458768 | tf_op jit(solution)/shard_map/reduce_scatter | solution.py:584
  1775.4 109.2 %all-reduce.33.cloned.1.call-done = (bf16[128]{0:T(256)(128)(2,1)}, bf16[128,128]{1,0:T(8,128)(2,1)}, bf16[128,128]{1,0:T(8,128)(2,1)}, bf16[128,24]{0,1:T(8,128...) async-done(((bf16[128]{0:T(256)(128)(2,1)}, ...) | async-done | bytes 74850 | tf_op jit(solution)/shard_map/psum | solution.py:625
  1898.1 116.4 %all-reduce.35.cloned.1.call-done = (bf16[128,512]{1,0:T(8,128)(2,1)}, bf16[64,1024]{1,0:T(8,128)(2,1)}, bf16[128,1536]{1,0:T(8,128)(2,1)}, bf16[128,1792]{1,0:T...) async-done(((bf16[128,512]{1,0:T(8,128)(2,1)}, bf16[64,1024]{1,0:T(8,128)(2,1)}, ...) | async-done | bytes 3080208 | tf_op jit(solution)/shard_map/psum | solution.py:626
  (653 shorter events, 436.8 us)
Async XLA Ops:
  7.3 206.3 %all-gather.25.cloned.1.call-start = ((), (), s32[]{:S(2)}) async-start(), calls=%async_computation.16 | async-start | bytes 4128768 | tf_op jit(solution)/shard_map/all_gather | solution.py:325
  8.0 260.8 %all-gather.21.cloned.1.call-start = ((), (), s32[]{:S(2)}) async-start(), calls=%async_computation.14 | async-start | bytes 1179648 | tf_op jit(solution)/shard_map/all_gather | solution.py:274
  8.8 263.0 %all-gather.19.cloned.1.call-start = ((), (), s32[]{:S(2)}) async-start(), calls=%async_computation.13 | async-start | bytes 1114112 | tf_op jit(solution)/shard_map/all_gather | solution.py:299
  93.7 187.9 %all-gather.23.cloned.1.call-start = ((), (), s32[]{:S(2)}) async-start(), calls=%async_computation.15 | async-start | bytes 1179648 | tf_op jit(solution)/shard_map/all_gather | solution.py:277
  94.3 202.3 %all-gather.37.cloned.1.call-start = ((), (), s32[]{:S(2)}) async-start(), calls=%async_computation.32 | async-start | bytes 13369344 | tf_op jit(solution)/shard_map/all_gather | solution.py:34
  227.3 198.2 %all-gather.29.cloned.1.call-start = ((), (), s32[]{:S(2)}) async-start(), calls=%async_computation.18 | async-start | bytes 3538944 | tf_op jit(solution)/shard_map/all_gather | solution.py:333
  228.0 269.7 %all-gather.31.cloned.1.call-start = ((), (), s32[]{:S(2)}) async-start(), calls=%async_computation.19 | async-start | bytes 4718592 | tf_op jit(solution)/shard_map/all_gather | solution.py:379
  228.8 340.6 %all-gather.33.cloned.1.call-start = ((), (), s32[]{:S(2)}) async-start(), calls=%async_computation.20 | async-start | bytes 4718592 | tf_op jit(solution)/shard_map/all_gather | solution.py:380
  229.5 411.4 %all-gather.35.cloned.1.call-start = ((), (), s32[]{:S(2)}) async-start(), calls=%async_computation.21 | async-start | bytes 4718592 | tf_op jit(solution)/shard_map/all_gather | solution.py:381
  230.1 501.8 %reduce-scatter.40.cloned.1.call-start = ((), (), s32[]{:S(2)}) async-start(), calls=%async_computation.34 | async-start | bytes 1114112
  686.1 218.4 %reduce-scatter.44.cloned.1.call-start = ((), (), s32[]{:S(2)}) async-start(), calls=%async_computation.36 | async-start | bytes 516096
  816.1 141.9 %reduce-scatter.42.cloned.1.call-start = ((), (), s32[]{:S(2)}) async-start(), calls=%async_computation.35 | async-start | bytes 294912
  821.8 209.8 %reduce-scatter.22.cloned.1.call-start = ((), (), s32[]{:S(2)}) async-start(), calls=%async_computation.23 | async-start | bytes 294912 | tf_op jit(solution)/shard_map/reduce_scatter | solution.py:572
  822.9 281.8 %reduce-scatter.24.cloned.1.call-start = ((), (), s32[]{:S(2)}) async-start(), calls=%async_computation.24 | async-start | bytes 294912 | tf_op jit(solution)/shard_map/reduce_scatter | solution.py:575
  824.0 356.3 %reduce-scatter.20.cloned.1.call-start = ((), (), s32[]{:S(2)}) async-start(), calls=%async_computation.22 | async-start | bytes 1179648 | tf_op jit(solution)/shard_map/reduce_scatter | solution.py:569
  826.4 429.0 %reduce-scatter.26.cloned.1.call-start = ((), (), s32[]{:S(2)}) async-start(), calls=%async_computation.25 | async-start | bytes 1179648 | tf_op jit(solution)/shard_map/reduce_scatter | solution.py:578
  827.9 511.3 %reduce-scatter.32.cloned.1.call-start = ((), (), s32[]{:S(2)}) async-start(), calls=%async_computation.28 | async-start | bytes 3538944 | tf_op jit(solution)/shard_map/reduce_scatter | solution.py:608
  830.7 590.8 %reduce-scatter.28.cloned.1.call-start = ((), (), s32[]{:S(2)}) async-start(), calls=%async_computation.26 | async-start | bytes 3538944 | tf_op jit(solution)/shard_map/reduce_scatter | solution.py:581
  833.5 676.0 %reduce-scatter.34.cloned.1.call-start = ((), (), s32[]{:S(2)}) async-start(), calls=%async_computation.29 | async-start | bytes 4718592 | tf_op jit(solution)/shard_map/reduce_scatter | solution.py:614
  837.2 760.2 %reduce-scatter.36.cloned.1.call-start = ((), (), s32[]{:S(2)}) async-start(), calls=%async_computation.30 | async-start | bytes 4718592 | tf_op jit(solution)/shard_map/reduce_scatter | solution.py:617
  841.5 843.9 %reduce-scatter.38.cloned.1.call-start = ((), (), s32[]{:S(2)}) async-start(), calls=%async_computation.31 | async-start | bytes 4718592 | tf_op jit(solution)/shard_map/reduce_scatter | solution.py:620
  846.0 924.8 %reduce-scatter.30.cloned.1.call-start = ((), (), s32[]{:S(2)}) async-start(), calls=%async_computation.27 | async-start | bytes 4128768 | tf_op jit(solution)/shard_map/reduce_scatter | solution.py:584
  856.2 1028.4 %all-reduce.33.cloned.1.call-start = ((), (), s32[]{:S(2)}) async-start(), calls=%async_computation.37 | async-start | bytes 154624 | tf_op jit(solution)/shard_map/psum | solution.py:625
  1104.7 909.7 %all-reduce.35.cloned.1.call-start = ((), (), s32[]{:S(2)}) async-start(), calls=%async_computation.38 | async-start | bytes 6160384 | tf_op jit(solution)/shard_map/psum | solution.py:626
  (170 other events, 4510.8 us)
Sparse Core Ops, SparseCore 0:
  10.4 72.6 all-gather.24
  85.5 46.5 all-gather.20
  170.8 46.3 all-gather.22
  226.8 69.7 all-gather.36
  298.8 62.9 all-gather.26
  364.1 61.3 all-gather.28
  427.8 69.8 all-gather.30
  500.1 69.2 all-gather.32
  571.6 69.2 all-gather.34
  675.9 55.9 reduce-scatter.39
  816.2 69.2 reduce-scatter.43
  888.9 69.0 reduce-scatter.41
  962.4 69.0 reduce-scatter.21
  1035.6 69.0 reduce-scatter.23
  1109.2 71.0 reduce-scatter.19
  1184.4 70.9 reduce-scatter.25
  1259.8 79.3 reduce-scatter.31
  1342.9 78.5 reduce-scatter.27
  1425.9 83.5 reduce-scatter.33
  1513.9 83.4 reduce-scatter.35
  1601.8 83.5 reduce-scatter.37
  1689.7 80.9 reduce-scatter.29
  1775.9 108.7 all-reduce.32
  1887.9 126.4 all-reduce.34
  (2 shorter events, 79.4 us)
where the time goes:
time: 2040 us; the launch traced here: 2030 us
  waiting for transfers between devices  1490 us (73%)
  blocking collectives  278 us (14%)
  matrix products  113 us (6%)
  other arithmetic  78.7 us (4%)
  local copies, waits for them, and re-layouts  37.8 us (2%)
  between operations  22.3 us (1%)
    psum x1, waiting for transfers between devices, local(): lax.psum(shard_query.astype(jnp.bfloat16), 'ctx').astype(jnp.float32)  116 us
    psum x1, waiting for transfers between devices, local(): lax.psum(shard_gain_one.astype(jnp.bfloat16), 'ctx').astype(jnp.float32)  109 us
    reduce_scatter x1, waiting for transfers between devices, local(): lax.psum_scatter(grad_w_down.astype(jnp.bfloat16), 'fsdp', scatter_dimens...  88 us
    reduce_scatter x1, waiting for transfers between devices, local(): lax.psum_scatter(grad_w_gate.astype(jnp.bfloat16), 'fsdp', scatter_dimens...  88 us
    reduce_scatter x1, waiting for transfers between devices, local(): lax.psum_scatter(grad_w_up.astype(jnp.bfloat16), 'fsdp', scatter_dimensio...  87.9 us
    reduce_scatter x1, waiting for transfers between devices, local(): lax.psum_scatter(grad_w_inner.astype(jnp.bfloat16), 'fsdp', scatter_dimen...  85.4 us
    reduce_scatter x1, waiting for transfers between devices, local(): lax.psum_scatter(grad_w_mixer_out.astype(jnp.bfloat16), 'fsdp', scatter_d...  83.8 us
    reduce_scatter x1, waiting for transfers between devices, local(): lax.psum_scatter(grad_w_gate_z.astype(jnp.bfloat16), 'fsdp', scatter_dime...  82.3 us
  transfers between devices with their start and end apart: 28, of which 23 were waited for; matrix products, arithmetic and copies ran while one was open for 7% of the time, Pallas kernels for 0%

commit v1 on v0

v1 whole, which is shorter than its diff:
```python
import jax
import jax.numpy as jnp
from jax import lax
from jax.experimental import pallas as pl
from jax.experimental.pallas import tpu as pltpu
from jax.sharding import PartitionSpec as P

HEADS = 8
KV_HEADS = 2
HEAD_DIM = 64
SSM_HEADS = 24
SSM_DIM = 64
STATE = 128
CONV = 4


epsilon = 1e-05
rope_base = 10000.0
key_scale = 0.5
attn_out_scale = 0.8
mixer_out_scale = 0.5
gate_scale = 0.75
down_scale = 0.8
masked_score = -1e30
highest = lax.Precision.HIGHEST


def matmul_f32(left_side, right_side):
    return jnp.dot(left_side, right_side, preferred_element_type=jnp.float32)


def right_trans(left_side, right_side):
    return lax.dot_general(
        left_side, right_side, (((1,), (1,)), ((), ())), preferred_element_type=jnp.float32
    )


def rms_scale(values, gain_vec):
    return (
        values * lax.rsqrt(jnp.mean(values * values, axis=-1, keepdims=True) + epsilon) * gain_vec
    )


def rope_tables(positions):
    half_dim = HEAD_DIM // 2
    inverse = rope_base ** (-jnp.arange(half_dim, dtype=jnp.float32) / half_dim)
    angles = positions.astype(jnp.float32)[:, None] * inverse[None, :]
    return (jnp.cos(angles)[:, None, :], jnp.sin(angles)[:, None, :])


def rotate(values, angle_cos, angle_sin):
    half_dim = values.shape[-1] // 2
    first_half = values[..., :half_dim]
    second_half = values[..., half_dim:]
    return jnp.concatenate(
        [
            first_half * angle_cos - second_half * angle_sin,
            second_half * angle_cos + first_half * angle_sin,
        ],
        axis=-1,
    )


def rotate_back(values, angle_cos, angle_sin):
    half_dim = values.shape[-1] // 2
    first_half = values[..., :half_dim]
    second_half = values[..., half_dim:]
    return jnp.concatenate(
        [
            first_half * angle_cos + second_half * angle_sin,
            second_half * angle_cos - first_half * angle_sin,
        ],
        axis=-1,
    )


def conv_mix(extended, seg_ext, seg_here, conv_weight, conv_bias):
    row_count = seg_here.shape[0]
    summed = jnp.broadcast_to(conv_bias[None, :], (row_count, conv_bias.shape[0]))
    for offset in range(conv_weight.shape[0]):
        same_doc = (seg_ext[offset : offset + row_count] == seg_here)[:, None]
        summed = summed + conv_weight[offset][None, :] * jnp.where(
            same_doc, extended[offset : offset + row_count], 0.0
        )
    return jax.nn.silu(summed)


def mixer_features(
    extended, seg_ext, seg_here, step_raw, conv_weight, conv_bias, step_bias, decay_log
):
    mixed_rows = conv_mix(extended, seg_ext, seg_here, conv_weight, conv_bias)
    row_count = seg_here.shape[0]
    width_inner = SSM_HEADS * SSM_DIM
    values_ssm = mixed_rows[:, :width_inner].reshape(row_count, SSM_HEADS, SSM_DIM)
    input_map = mixed_rows[:, width_inner : width_inner + STATE]
    output_map = mixed_rows[:, width_inner + STATE :]
    step_size = jax.nn.softplus(step_raw + step_bias[None, :])
    log_decay = -step_size * jnp.exp(decay_log)[None, :]
    return (values_ssm, input_map, output_map, step_size, log_decay)


def ssd_states(values_ssm, input_map, step_size, log_decay, seg_here, seg_before):
    cumulative = jnp.cumsum(log_decay, axis=0)
    last_seg = seg_here[-1]
    tail_weight = (
        jnp.where(
            (seg_here == last_seg)[:, None], jnp.exp(cumulative[-1][None, :] - cumulative), 0.0
        )
        * step_size
    )
    weighted = tail_weight[:, :, None] * values_ssm
    block_state = jnp.einsum("shp,sn->phn", weighted, input_map, precision=highest)
    block_decay = jnp.exp(cumulative[-1]) * (last_seg == seg_before).astype(jnp.float32)
    return (block_decay, block_state)


def ssd_output(
    values_ssm,
    input_map,
    output_map,
    step_size,
    log_decay,
    seg_here,
    seg_before,
    skip_gain,
    carried,
):
    row_count = seg_here.shape[0]
    cumulative = jnp.cumsum(log_decay, axis=0)
    order_idx = jnp.arange(row_count, dtype=jnp.int32)
    causal_same = (seg_here[:, None] == seg_here[None, :]) & (
        order_idx[:, None] >= order_idx[None, :]
    )
    keep_mask = causal_same[:, :, None]
    spread = cumulative[:, None, :] - cumulative[None, :, :]
    decay_mat = jnp.where(keep_mask, jnp.exp(jnp.where(keep_mask, spread, 0.0)), 0.0)
    pairing = jnp.dot(output_map, input_map.T, precision=highest)
    mixing = decay_mat * pairing[:, :, None] * step_size[None, :, :]
    result = jnp.einsum("tsh,shp->thp", mixing, values_ssm, precision=highest)
    entering = jnp.exp(cumulative) * (seg_here == seg_before).astype(jnp.float32)[:, None]
    result = result + entering[:, :, None] * jnp.einsum(
        "tn,phn->thp", output_map, carried, precision=highest
    )
    return (result + skip_gain[None, :, None] * values_ssm, entering)


def gate_norm(result, gate_z, mixer_gain):
    flat_rows = result.reshape(gate_z.shape) * jax.nn.silu(gate_z)
    return rms_scale(flat_rows, mixer_gain)


def head_forward(query_head, key_head, value_head, visible):
    scores = jnp.einsum("tgd,jd->gtj", query_head, key_head, preferred_element_type=jnp.float32)
    scores = jnp.where(visible[None], scores, masked_score)
    row_max = jnp.max(scores, axis=-1, keepdims=True)
    exp_scores = jnp.exp(scores - row_max)
    row_sum = jnp.sum(exp_scores, axis=-1, keepdims=True)
    prob_low = (exp_scores / row_sum).astype(jnp.bfloat16)
    attended = jnp.einsum("gtj,jd->tgd", prob_low, value_head, preferred_element_type=jnp.float32)
    return (attended, (row_max + jnp.log(row_sum))[..., 0])


def head_backward(query_head, key_head, value_head, grad_head, log_total, visible):
    scores = jnp.einsum("tgd,jd->gtj", query_head, key_head, preferred_element_type=jnp.float32)
    scores = jnp.where(visible[None], scores, masked_score)
    prob_full = jnp.where(visible[None], jnp.exp(scores - log_total[..., None]), 0.0)
    prob_low = prob_full.astype(jnp.bfloat16)
    grad_probs = jnp.einsum(
        "tgd,jd->gtj", grad_head, value_head, preferred_element_type=jnp.float32
    )
    inner_sum = jnp.sum(prob_full * grad_probs, axis=-1, keepdims=True)
    grad_scores = (prob_full * (grad_probs - inner_sum)).astype(jnp.bfloat16)
    grad_query = jnp.einsum(
        "gtj,jd->tgd", grad_scores, key_head, preferred_element_type=jnp.float32
    )
    grad_key = jnp.einsum(
        "gtj,tgd->jd", grad_scores, query_head, preferred_element_type=jnp.float32
    )
    grad_value = jnp.einsum("gtj,tgd->jd", prob_low, grad_head, preferred_element_type=jnp.float32)
    return (grad_query, grad_key, grad_value)


MESH = pl.DeviceIdType.MESH
CTX = 16
FSDP = 8
COLS = 4224
PAD_AT = 4096
CUT_COLS = 1792
CUT_ROWS = 192
OUT_ROWS = 512
HALF = 512
QUARTER = 32
QUARTER_A = CUT_ROWS // 4
QUARTER_B = (OUT_ROWS - CUT_ROWS) // 4
SMALL = 1577
CHUNK = SSM_DIM * SSM_HEADS // CTX
VMEM_LIMIT = 60 * 2**20


def place():
    f, c = lax.axis_index("fsdp"), lax.axis_index("ctx")
    return f, c, c // 4, (c // 2) % 2, c % 2


def at_ctx(y, low_z, core):
    return (y * 2 + low_z) * 2 + core


def meet(partners):
    barrier = pltpu.get_barrier_semaphore()
    for partner in partners:
        pl.semaphore_signal(barrier, inc=1, device_id=partner, device_id_type=MESH)
    pl.semaphore_wait(barrier, len(partners))


class Sender:
    def __init__(self, send_sem, recv_sem):
        self.send_sem, self.recv_sem, self.used, self.all = send_sem, recv_sem, 0, []

    def push(self, src, dst, partner):
        index = self.used
        self.used += 1
        copy = pltpu.make_async_remote_copy(
            src_ref=src,
            dst_ref=dst,
            send_sem=self.send_sem.at[index],
            recv_sem=self.recv_sem.at[index],
            device_id=partner,
            device_id_type=MESH,
        )
        copy.start()
        self.all.append(copy)
        return copy

    def drain(self):
        for copy in self.all:
            copy.wait_send()


def call_kernel(body, name, cid, outs, ins, sems, scratch=(), space=pltpu.VMEM, cost=0):
    return pl.pallas_call(
        body,
        name=name,
        out_shape=outs,
        in_specs=[pl.BlockSpec(memory_space=space)] * len(ins),
        out_specs=jax.tree.map(lambda _: pl.BlockSpec(memory_space=space), outs),
        scratch_shapes=[
            *scratch,
            pltpu.SemaphoreType.DMA((sems,)),
            pltpu.SemaphoreType.DMA((sems,)),
        ],
        compiler_params=pltpu.CompilerParams(
            collective_id=cid, has_side_effects=True, vmem_limit_bytes=VMEM_LIMIT
        ),
    )(*ins)


def shape_of(dims, kind):
    return jax.ShapeDtypeStruct(dims, kind)


def gather_body(in12, in3, out12, out3, own_sem, send_sem, recv_sem):
    f, c, y, low_z, core = place()
    peers = [{"fsdp": (f + d) % FSDP} for d in range(1, FSDP)]
    sources = [(f + FSDP - d) % FSDP for d in range(1, FSDP)]
    columns = [{"ctx": at_ctx((y + e) % 4, low_z, core)} for e in range(1, 4)]
    sibling = {"ctx": at_ctx(y, low_z, 1 - core)}
    meet(peers + columns + [sibling])
    net = Sender(send_sem, recv_sem)
    own = [
        pltpu.make_async_copy(in12.at[0], out12.at[0, f], own_sem.at[0]),
        pltpu.make_async_copy(in12.at[1], out12.at[1, f], own_sem.at[1]),
        pltpu.make_async_copy(in3, out3.at[f], own_sem.at[2]),
    ]
    half = pl.ds(pl.multiple_of(core * HALF, HALF), HALF)
    strip = pl.ds(pl.multiple_of(y * QUARTER, QUARTER), QUARTER)
    strip3 = pl.ds(pl.multiple_of(CUT_ROWS + y * QUARTER_B, 16), QUARTER_B)
    right = pl.ds(CUT_COLS, COLS - CUT_COLS)
    left = pl.ds(0, CUT_COLS)
    top = pl.ds(0, CUT_ROWS)
    below = pl.ds(CUT_ROWS, OUT_ROWS - CUT_ROWS)
    part_b = [
        (
            net.push(in12.at[core, strip, right], out12.at[core, f, strip, right], peer),
            net.push(in3.at[strip3, half], out3.at[f, strip3, half], peer),
        )
        for peer in peers
    ]
    part_a = [
        (
            net.push(in12.at[core, :, left], out12.at[core, f, :, left], peer),
            net.push(in3.at[top, half], out3.at[f, top, half], peer),
        )
        for peer in peers
    ]
    for copy in own:
        copy.start()
    passed = []
    for index, source in enumerate(sources):
        for copy in part_b[index]:
            copy.wait_recv()
        one, two = out12.at[core, source, strip, right], out3.at[source, strip3, half]
        passed.append([(net.push(one, one, to), net.push(two, two, to)) for to in columns])
    crossing = []
    for index, source in enumerate(sources):
        for copy in part_a[index]:
            copy.wait_recv()
        one, two = out12.at[core, source, :, left], out3.at[source, top, half]
        crossing += [net.push(one, one, sibling), net.push(two, two, sibling)]
    for index, source in enumerate(sources):
        for pair in passed[index]:
            for copy in pair:
                copy.wait_recv()
        one, two = out12.at[core, source, :, right], out3.at[source, below, half]
        crossing += [net.push(one, one, sibling), net.push(two, two, sibling)]
    for copy in crossing:
        copy.wait_recv()
    net.drain()
    for copy in own:
        copy.wait()


def gather_weights(in12, in3):
    return call_kernel(
        gather_body,
        "gather_weights",
        0,
        (
            shape_of((2, FSDP, 128, COLS), jnp.bfloat16),
            shape_of((FSDP, OUT_ROWS, 2 * HALF), jnp.bfloat16),
        ),
        (in12, in3),
        98,
        (pltpu.SemaphoreType.DMA((3,)),),
        pl.ANY,
    )


def ctx_peers(c):
    return [{"ctx": (c + e) % CTX} for e in range(1, CTX)]


def keys_body(kv, rim, seg, kv_all, rim_out, seg_all, send_sem, recv_sem):
    f, c, y, low_z, core = place()
    peers = ctx_peers(c)
    meet(peers)
    net = Sender(send_sem, recv_sem)
    copies = [net.push(rim, rim_out, peers[0])]
    for peer in peers:
        copies.append(net.push(kv, kv_all.at[c], peer))
        copies.append(net.push(seg, seg_all.at[c], peer))
    kv_all[c] = kv[...]
    seg_all[c] = seg[...]
    for copy in copies:
        copy.wait_recv()
    net.drain()


def gather_keys(kv, rim, seg):
    return call_kernel(
        keys_body,
        "gather_keys",
        1,
        (
            shape_of((CTX, *kv.shape), kv.dtype),
            shape_of(rim.shape, rim.dtype),
            shape_of((CTX, *seg.shape), seg.dtype),
        ),
        (kv, rim, seg),
        31,
    )


def scan_rows(order, decay_of, parts, carries):
    state = jnp.zeros((CHUNK, STATE), jnp.float32)
    for at in order:
        carries[at] = state.astype(jnp.bfloat16)
        decay = decay_of[at]
        whole = jnp.concatenate([decay] * (CHUNK // SSM_HEADS), axis=0)
        state = whole * state + parts[at].astype(jnp.float32)


def send_back(net, c, peers, carries, carried):
    copies = [
        net.push(carries.at[(c + e + 1) % CTX], carried.at[c], peer) for e, peer in enumerate(peers)
    ]
    carried[c] = carries[c]
    for copy in copies:
        copy.wait_recv()
    net.drain()


def forward_body(states, decay, carried, decays, parts, carries, send_sem, recv_sem):
    f, c, y, low_z, core = place()
    peers = ctx_peers(c)
    meet(peers)
    net = Sender(send_sem, recv_sem)
    copies = []
    for e, peer in enumerate(peers):
        copies.append(net.push(states.at[(c + e + 1) % CTX], parts.at[c], peer))
        copies.append(net.push(decay, decays.at[c], peer))
    parts[c] = states[c]
    decays[c] = decay[...]
    for copy in copies:
        copy.wait_recv()
    scan_rows(range(CTX), decays, parts, carries)
    send_back(net, c, peers, carries, carried)


def backward_body(states, decays, carried, parts, carries, send_sem, recv_sem):
    f, c, y, low_z, core = place()
    peers = ctx_peers(c)
    meet(peers)
    net = Sender(send_sem, recv_sem)
    copies = [
        net.push(states.at[(c + e + 1) % CTX], parts.at[c], peer) for e, peer in enumerate(peers)
    ]
    parts[c] = states[c]
    for copy in copies:
        copy.wait_recv()
    scan_rows(range(CTX - 1, -1, -1), decays, parts, carries)
    send_back(net, c, peers, carries, carried)


def scan_forward(states, decay):
    chunks = states.astype(jnp.bfloat16).reshape(CTX, CHUNK, STATE)
    wide = jnp.broadcast_to(decay[:, None], (SSM_HEADS, STATE))
    carried, decays = call_kernel(
        forward_body,
        "scan_forward",
        2,
        (
            shape_of((CTX, CHUNK, STATE), jnp.bfloat16),
            shape_of((CTX, SSM_HEADS, STATE), jnp.float32),
        ),
        (chunks, wide),
        45,
        (pltpu.VMEM((CTX, CHUNK, STATE), jnp.bfloat16),) * 2,
    )
    return carried.reshape(SSM_DIM, SSM_HEADS, STATE).astype(jnp.float32), decays


def scan_backward(states, decays):
    chunks = states.astype(jnp.bfloat16).reshape(CTX, CHUNK, STATE)
    carried = call_kernel(
        backward_body,
        "scan_backward",
        3,
        shape_of((CTX, CHUNK, STATE), jnp.bfloat16),
        (chunks, decays),
        30,
        (pltpu.VMEM((CTX, CHUNK, STATE), jnp.bfloat16),) * 2,
    )
    return carried.reshape(SSM_DIM, SSM_HEADS, STATE).astype(jnp.float32)


def key_grads_body(terms, rim, total, rim_out, parts, send_sem, recv_sem):
    f, c, y, low_z, core = place()
    peers = ctx_peers(c)
    meet(peers)
    net = Sender(send_sem, recv_sem)
    copies = [net.push(rim, rim_out, peers[-1])]
    for e, peer in enumerate(peers):
        copies.append(net.push(terms.at[(c + e + 1) % CTX], parts.at[e], peer))
    for copy in copies:
        copy.wait_recv()
    summed = terms[c].astype(jnp.float32)
    for e in range(CTX - 1):
        summed = summed + parts[e].astype(jnp.float32)
    total[...] = summed
    net.drain()


def sum_key_grads(terms, rim):
    return call_kernel(
        key_grads_body,
        "sum_key_grads",
        4,
        (shape_of(terms.shape[1:], jnp.float32), shape_of(rim.shape, rim.dtype)),
        (terms, rim),
        16,
        (pltpu.VMEM((CTX - 1, *terms.shape[1:]), terms.dtype),),
    )


def dot_rows(left, right):
    return lax.dot_general(
        left, right, (((0,), (0,)), ((), ())), preferred_element_type=jnp.float32
    ).astype(jnp.bfloat16)


def weight_grads_body(
    norms,
    grads12,
    acts,
    grads3,
    small,
    out12,
    out3,
    both_norm,
    both12,
    both_act,
    both3,
    small_in,
    own12,
    own3,
    a_in12,
    a_in3,
    y_in12,
    y_in3,
    mid12,
    mid3,
    f_in12,
    f_in3,
    full12,
    full3,
    ya_in12,
    ya_in3,
    z_out12,
    z_out3,
    z_in12,
    z_in3,
    send_sem,
    recv_sem,
):
    f, c, y, low_z, core = place()
    toks = norms.shape[1]
    columns = [(y + e) % 4 for e in range(1, 4)]
    to_y = [{"ctx": at_ctx(q, low_z, core)} for q in columns]
    sibling = {"ctx": at_ctx(y, low_z, 1 - core)}
    over_z = {"ctx": at_ctx(y, 1 - low_z, core)}
    peers = [{"fsdp": (f + d) % FSDP} for d in range(1, FSDP)]
    meet(peers + to_y + [sibling, over_z])
    net = Sender(send_sem.at[pl.ds(14, 64)], recv_sem.at[pl.ds(14, 64)])
    half = pl.ds(pl.multiple_of(core * HALF, HALF), HALF)
    other_half = pl.ds(pl.multiple_of((1 - core) * HALF, HALF), HALF)
    here, there = pl.ds(0, toks), pl.ds(toks, toks)
    first = [
        net.push(norms.at[1 - core], both_norm.at[there], sibling),
        net.push(grads12.at[1 - core], both12.at[there], sibling),
        net.push(acts, both_act.at[:, there], sibling),
        net.push(grads3.at[:, :, other_half], both3.at[:, there], sibling),
        net.push(small, small_in, sibling),
    ]
    both_norm[here] = norms[core]
    both12[here] = grads12[core]
    both_act[:, here] = acts[...]
    both3[:, here] = grads3[:, :, half]
    for copy in first:
        copy.wait_recv()

    def block(owner):
        features = both_norm[:, pl.ds(pl.multiple_of(owner * 128, 128), 128)]
        for piece in range(3):
            wide = COLS // 3
            at = pl.ds(piece * wide, wide)
            own12[owner, :, at] = dot_rows(features, both12[:, at])
        extra = (small[owner] + small_in[owner]) * core.astype(jnp.float32)
        tail = own12[owner, 0:16, PAD_AT:COLS].astype(jnp.float32)
        own12[owner, 0:16, PAD_AT:COLS] = (tail + extra).astype(jnp.bfloat16)
        own3[owner, 0:64] = dot_rows(both_act[owner, :, 0:64], both3[0])
        own3[owner, 64:256] = dot_rows(both_act[owner, :, 64:256], both3[1])
        own3[owner, 256:512] = dot_rows(both_act[owner, :, 256:512], both3[2])

    def a_copies(d, owner):
        peer = {"fsdp": owner}
        return [
            pltpu.make_async_remote_copy(
                src_ref=src,
                dst_ref=dst,
                send_sem=send_sem.at[2 * d + k],
                recv_sem=recv_sem.at[2 * d + k],
                device_id=peer,
                device_id_type=MESH,
            )
            for k, (src, dst) in enumerate(
                (
                    (own12.at[owner, :, pl.ds(0, CUT_COLS)], a_in12.at[d]),
                    (own3.at[owner, pl.ds(0, CUT_ROWS)], a_in3.at[d]),
                )
            )
        ]

    def turn(d, nothing):
        owner = (f + d + 1) % FSDP
        block(owner)
        for copy in a_copies(d, owner):
            copy.start()
        return nothing

    lax.fori_loop(0, FSDP - 1, turn, 0)
    block(f)
    right = pl.ds(CUT_COLS, COLS - CUT_COLS)
    by_y = []
    for e, q in enumerate(columns):
        rows = pl.ds(pl.multiple_of(q * QUARTER, QUARTER), QUARTER)
        rows3 = pl.ds(pl.multiple_of(CUT_ROWS + q * QUARTER_B, 16), QUARTER_B)
        by_y.append(net.push(own12.at[:, rows, right], y_in12.at[e], to_y[e]))
        by_y.append(net.push(own3.at[:, rows3], y_in3.at[e], to_y[e]))
    for copy in by_y:
        copy.wait_recv()

    def middle(owner, nothing):
        rows = pl.ds(pl.multiple_of(y * QUARTER, QUARTER), QUARTER)
        rows3 = pl.ds(pl.multiple_of(CUT_ROWS + y * QUARTER_B, 16), QUARTER_B)
        total = own12[owner, rows, CUT_COLS:COLS].astype(jnp.float32)
        total3 = own3[owner, rows3].astype(jnp.float32)
        for e in range(3):
            total = total + y_in12[e, owner].astype(jnp.float32)
            total3 = total3 + y_in3[e, owner].astype(jnp.float32)
        mid12[owner] = total.astype(jnp.bfloat16)
        mid3[owner] = total3.astype(jnp.bfloat16)
        return nothing

    lax.fori_loop(0, FSDP, middle, 0)
    by_f = []
    for d in range(FSDP - 1):
        owner = (f + d + 1) % FSDP
        by_f.append(net.push(mid12.at[owner], f_in12.at[d], peers[d]))
        by_f.append(net.push(mid3.at[owner], f_in3.at[d], peers[d]))
    for d in range(FSDP - 1):
        for copy in a_copies(d, (f + d + 1) % FSDP):
            copy.wait_recv()

    def whole(q, nothing):
        rows = pl.ds(pl.multiple_of(q * QUARTER, QUARTER), QUARTER)
        rows3 = pl.ds(pl.multiple_of(q * QUARTER_A, 16), QUARTER_A)
        total = own12[f, rows, 0:CUT_COLS].astype(jnp.float32)
        total3 = own3[f, rows3].astype(jnp.float32)
        for d in range(FSDP - 1):
            total = total + a_in12[d, rows].astype(jnp.float32)
            total3 = total3 + a_in3[d, rows3].astype(jnp.float32)
        full12[q] = total.astype(jnp.bfloat16)
        full3[q] = total3.astype(jnp.bfloat16)
        return nothing

    lax.fori_loop(0, 4, whole, 0)
    by_ya = []
    for e, q in enumerate(columns):
        by_ya.append(net.push(full12.at[q], ya_in12.at[e], to_y[e]))
        by_ya.append(net.push(full3.at[q], ya_in3.at[e], to_y[e]))
    for copy in by_f:
        copy.wait_recv()
    total = mid12[f].astype(jnp.float32)
    total3 = mid3[f].astype(jnp.float32)
    for d in range(FSDP - 1):
        total = total + f_in12[d].astype(jnp.float32)
        total3 = total3 + f_in3[d].astype(jnp.float32)
    z_out12[:, CUT_COLS:COLS] = total.astype(jnp.bfloat16)
    z_out3[QUARTER_A:] = total3.astype(jnp.bfloat16)
    for copy in by_ya:
        copy.wait_recv()
    total = full12[y].astype(jnp.float32)
    total3 = full3[y].astype(jnp.float32)
    for e in range(3):
        total = total + ya_in12[e].astype(jnp.float32)
        total3 = total3 + ya_in3[e].astype(jnp.float32)
    z_out12[:, 0:CUT_COLS] = total.astype(jnp.bfloat16)
    z_out3[0:QUARTER_A] = total3.astype(jnp.bfloat16)
    swap = [net.push(z_out12, z_in12, over_z), net.push(z_out3, z_in3, over_z)]
    for copy in swap:
        copy.wait_recv()
    mine = pl.ds(pl.multiple_of(y * QUARTER, QUARTER), QUARTER)
    mine_a = pl.ds(pl.multiple_of(y * QUARTER_A, 16), QUARTER_A)
    mine_b = pl.ds(pl.multiple_of(CUT_ROWS + y * QUARTER_B, 16), QUARTER_B)
    out12[core, mine] = (
        z_out12[...].astype(jnp.float32) + z_in12[...].astype(jnp.float32)
    ).astype(jnp.bfloat16)
    total3 = (z_out3[...].astype(jnp.float32) + z_in3[...].astype(jnp.float32)).astype(jnp.bfloat16)
    out3[mine_a, half] = total3[:QUARTER_A]
    out3[mine_b, half] = total3[QUARTER_A:]
    spread = []
    for to in to_y:
        for ref in (out12.at[core, mine], out3.at[mine_a, half], out3.at[mine_b, half]):
            spread.append(net.push(ref, ref, to))
    for copy in spread:
        copy.wait_recv()
    last = [
        net.push(out12.at[core], out12.at[core], sibling),
        net.push(out3.at[:, half], out3.at[:, half], sibling),
    ]
    for copy in last:
        copy.wait_recv()
    for d in range(FSDP - 1):
        for copy in a_copies(d, (f + d + 1) % FSDP):
            copy.wait_send()
    net.drain()


def sum_weight_grads(norms, grads12, acts, grads3, small):
    toks = norms.shape[1]
    low = jnp.bfloat16
    right, below = COLS - CUT_COLS, OUT_ROWS - CUT_ROWS
    scratch = [
        ((2 * toks, 1024), low),
        ((2 * toks, COLS), low),
        ((FSDP, 2 * toks, HALF), low),
        ((3, 2 * toks, HALF), low),
        (small.shape, jnp.float32),
        ((FSDP, 128, COLS), low),
        ((FSDP, OUT_ROWS, HALF), low),
        ((FSDP - 1, 128, CUT_COLS), low),
        ((FSDP - 1, CUT_ROWS, HALF), low),
        ((3, FSDP, QUARTER, right), low),
        ((3, FSDP, QUARTER_B, HALF), low),
        ((FSDP, QUARTER, right), low),
        ((FSDP, QUARTER_B, HALF), low),
        ((FSDP - 1, QUARTER, right), low),
        ((FSDP - 1, QUARTER_B, HALF), low),
        ((4, QUARTER, CUT_COLS), low),
        ((4, QUARTER_A, HALF), low),
        ((3, QUARTER, CUT_COLS), low),
        ((3, QUARTER_A, HALF), low),
        ((QUARTER, COLS), low),
        ((QUARTER_A + QUARTER_B, HALF), low),
        ((QUARTER, COLS), low),
        ((QUARTER_A + QUARTER_B, HALF), low),
    ]
    return call_kernel(
        weight_grads_body,
        "sum_weight_grads",
        5,
        (shape_of((2, 128, COLS), low), shape_of((OUT_ROWS, 2 * HALF), low)),
        (norms, grads12, acts, grads3, small),
        80,
        [pltpu.VMEM(dims, kind) for dims, kind in scratch],
    )


def local(
    layer_input,
    segment_ids,
    norm_gain,
    w_query,
    w_key,
    w_value,
    w_attn_out,
    w_gate_z,
    w_inner,
    w_step,
    conv_weight,
    conv_bias,
    step_bias,
    decay_log,
    skip_gain,
    mixer_gain,
    w_mixer_out,
    ffn_gain,
    w_gate,
    w_up,
    w_down,
    out_grad,
):
    low = jnp.bfloat16
    tok_rows = layer_input.shape[1]
    ctx_here = lax.axis_index("ctx")
    first_pos = ctx_here * tok_rows
    seg_here = segment_ids[0]
    pos_here = first_pos + jnp.arange(tok_rows, dtype=jnp.int32)
    residual_in = layer_input[0].astype(jnp.float32)
    grad_final = out_grad[0].astype(jnp.float32)
    group_size = HEADS // KV_HEADS
    kv_width = KV_HEADS * HEAD_DIM
    q_width = HEADS * HEAD_DIM
    width_inner = SSM_HEADS * SSM_DIM
    conv_width = width_inner + 2 * STATE
    z_at = q_width + 2 * kv_width
    inner_at = z_at + width_inner
    step_at = inner_at + conv_width

    small = jnp.concatenate(
        [
            norm_gain,
            conv_weight.reshape(-1),
            conv_bias,
            step_bias,
            decay_log,
            skip_gain,
            mixer_gain,
            ffn_gain,
            jnp.zeros((2048 - SMALL,), low),
        ]
    ).reshape(16, 128)
    in_one = jnp.concatenate(
        [w_query, w_key, w_value, w_gate_z, w_inner, jnp.pad(w_step, ((0, 0), (0, 104)))], axis=1
    )
    in_two = jnp.concatenate([w_gate, w_up, jnp.pad(small, ((0, 112), (0, 0)))], axis=1)
    in_three = jnp.concatenate([w_attn_out, w_mixer_out, w_down], axis=0)
    all12, all3 = gather_weights(jnp.stack([in_one, in_two]), in_three)
    full_one = all12[0].reshape(FSDP * 128, COLS)
    full_two = all12[1].reshape(FSDP * 128, COLS)
    attn_out_full = all3[:, 0:64].reshape(q_width, -1)
    mixer_out_full = all3[:, 64:256].reshape(width_inner, -1)
    down_full = all3[:, 256:512].reshape(FSDP * 256, -1)
    smalls = all12[1, :, 0:16, PAD_AT:COLS].reshape(FSDP, 2048).astype(jnp.float32)
    gain_one_f = smalls[:, 0:128].reshape(-1)
    conv_f = (
        smalls[:, 128:1024].reshape(FSDP, CONV, 224).transpose(1, 0, 2).reshape(CONV, conv_width)
    )
    conv_bias_f = smalls[:, 1024:1248].reshape(-1)
    step_bias_f = smalls[:, 1248:1251].reshape(-1)
    decay_f = smalls[:, 1251:1254].reshape(-1)
    skip_f = smalls[:, 1254:1257].reshape(-1)
    mixer_gain_f = smalls[:, 1257:1449].reshape(-1)
    gain_two_f = smalls[:, 1449:1577].reshape(-1)

    normed_low = rms_scale(residual_in, gain_one_f).astype(low)
    angle_cos, angle_sin = rope_tables(pos_here)
    projected = matmul_f32(normed_low, full_one)
    query_rot = rotate(
        projected[:, :q_width].reshape(tok_rows, HEADS, HEAD_DIM), angle_cos, angle_sin
    ) * HEAD_DIM ** (-0.5)
    key_rot = (
        rotate(
            projected[:, q_width : q_width + kv_width].reshape(tok_rows, KV_HEADS, HEAD_DIM),
            angle_cos,
            angle_sin,
        )
        * key_scale
    )
    value_proj = projected[:, q_width + kv_width : z_at]
    gate_z = projected[:, z_at:inner_at]
    inner_pre = projected[:, inner_at:step_at]
    step_raw = projected[:, step_at : step_at + SSM_HEADS]
    query_low = query_rot.astype(low)
    local_kv = jnp.concatenate(
        [key_rot.reshape(tok_rows, kv_width).astype(low), value_proj.astype(low)], axis=1
    )
    kv_all, rim_got, seg_got = gather_keys(
        local_kv, inner_pre[tok_rows - 8 :], jnp.broadcast_to(segment_ids, (8, tok_rows))
    )
    seq_total = CTX * tok_rows
    pos_all = jnp.arange(seq_total, dtype=jnp.int32)
    seg_all = seg_got[:, 0].reshape(seq_total)
    kv_all = kv_all.reshape(seq_total, 2 * kv_width)
    key_heads = kv_all[:, :kv_width].reshape(seq_total, KV_HEADS, HEAD_DIM).transpose(1, 0, 2)
    value_heads = kv_all[:, kv_width:].reshape(seq_total, KV_HEADS, HEAD_DIM).transpose(1, 0, 2)
    query_heads = query_low.reshape(tok_rows, KV_HEADS, group_size, HEAD_DIM).transpose(1, 0, 2, 3)
    visible = (pos_all[None, :] <= pos_here[:, None]) & (seg_all[None, :] == seg_here[:, None])
    attended, log_total = lax.map(
        lambda head_parts: head_forward(head_parts[0], head_parts[1], head_parts[2], visible),
        (query_heads, key_heads, value_heads),
    )
    attn_low = attended.transpose(1, 0, 2, 3).reshape(tok_rows, q_width).astype(low)
    attn_branch = matmul_f32(attn_low, attn_out_full) * attn_out_scale

    rim_rows = CONV - 1
    rim_in = jnp.where(ctx_here > 0, rim_got[8 - rim_rows :], 0.0)
    extended = jnp.concatenate([rim_in, inner_pre], axis=0)
    rim_start = jnp.maximum(first_pos - rim_rows, 0)
    seg_rim = lax.dynamic_slice_in_dim(seg_all, rim_start, rim_rows)
    seg_ext = jnp.concatenate([seg_rim, seg_here])
    seg_prior = lax.dynamic_index_in_dim(seg_all, jnp.maximum(first_pos - 1, 0), keepdims=False)
    seg_before = jnp.where(ctx_here > 0, seg_prior, -1)
    values_ssm, input_map, output_map, step_size, log_decay = mixer_features(
        extended, seg_ext, seg_here, step_raw, conv_f, conv_bias_f, step_bias_f, decay_f
    )
    block_decay, block_state = ssd_states(
        values_ssm, input_map, step_size, log_decay, seg_here, seg_before
    )
    carried, decays = scan_forward(block_state, block_decay)
    mixer_result, entering = ssd_output(
        values_ssm,
        input_map,
        output_map,
        step_size,
        log_decay,
        seg_here,
        seg_before,
        skip_f,
        carried,
    )
    mixer_low = gate_norm(mixer_result, gate_z, mixer_gain_f).astype(low)
    mixer_branch = matmul_f32(mixer_low, mixer_out_full) * mixer_out_scale
    middle = residual_in + attn_branch + mixer_branch
    normed_two_low = rms_scale(middle, gain_two_f).astype(low)
    both_pre = matmul_f32(normed_two_low, full_two)
    ff_width = FSDP * 256
    gate_pre = both_pre[:, :ff_width] * gate_scale
    up_pre = both_pre[:, ff_width : 2 * ff_width]
    hidden_low = (jax.nn.silu(gate_pre) * up_pre).astype(low)
    layer_out = middle + matmul_f32(hidden_low, down_full) * down_scale

    grad_down_in = (grad_final * down_scale).astype(low)
    grad_hidden = right_trans(grad_down_in, down_full)
    gate_sig = jax.nn.sigmoid(gate_pre)
    grad_gate_in = (
        grad_hidden * up_pre * gate_sig * (1.0 + gate_pre * (1.0 - gate_sig)) * gate_scale
    ).astype(low)
    grad_up_in = (grad_hidden * gate_pre * gate_sig).astype(low)
    grads_two = jnp.concatenate(
        [grad_gate_in, grad_up_in, jnp.zeros((tok_rows, COLS - PAD_AT), low)], axis=1
    )
    grad_normed_two = right_trans(grads_two, full_two)
    _, pull_two = jax.vjp(rms_scale, middle, gain_two_f)
    grad_mid_norm, grad_gain_two = pull_two(grad_normed_two)
    grad_middle = grad_final + grad_mid_norm
    grad_mixer_in = (grad_middle * mixer_out_scale).astype(low)
    grad_mixer_normed = right_trans(grad_mixer_in, mixer_out_full)
    _, pull_gate = jax.vjp(gate_norm, mixer_result, gate_z, mixer_gain_f)
    grad_result, grad_gate_z, grad_mixer_gain = pull_gate(grad_mixer_normed)
    grad_weighted = grad_result * entering[:, :, None]
    grad_carried = jnp.einsum("thp,tn->phn", grad_weighted, output_map, precision=highest)
    grad_out_state = scan_backward(grad_carried, decays)
    grad_block_decay = jnp.sum(grad_out_state * carried, axis=(0, 2))

    def mixer_core(
        core_ext,
        core_step,
        core_conv,
        core_conv_bias,
        core_step_bias,
        core_decay,
        core_skip,
        core_carried,
    ):
        core_values, core_input, core_output, core_size, core_log = mixer_features(
            core_ext,
            seg_ext,
            seg_here,
            core_step,
            core_conv,
            core_conv_bias,
            core_step_bias,
            core_decay,
        )
        core_block_decay, core_block_state = ssd_states(
            core_values, core_input, core_size, core_log, seg_here, seg_before
        )
        core_result, _ = ssd_output(
            core_values,
            core_input,
            core_output,
            core_size,
            core_log,
            seg_here,
            seg_before,
            core_skip,
            core_carried,
        )
        return (core_result, core_block_decay, core_block_state)

    _, pull_core = jax.vjp(
        mixer_core, extended, step_raw, conv_f, conv_bias_f, step_bias_f, decay_f, skip_f, carried
    )
    grad_ext, grad_step_raw, grad_conv, grad_conv_bias, grad_step_bias, grad_decay, grad_skip, _ = (
        pull_core((grad_result, grad_block_decay, grad_out_state))
    )

    grad_attn_in = (grad_middle * attn_out_scale).astype(low)
    grad_attended = right_trans(grad_attn_in, attn_out_full).astype(low)
    grad_heads = grad_attended.reshape(tok_rows, KV_HEADS, group_size, HEAD_DIM).transpose(
        1, 0, 2, 3
    )
    grad_query_h, grad_key_h, grad_value_h = lax.map(
        lambda head_parts: head_backward(
            head_parts[0], head_parts[1], head_parts[2], head_parts[3], head_parts[4], visible
        ),
        (query_heads, key_heads, value_heads, grad_heads, log_total),
    )
    grad_kv_terms = jnp.concatenate(
        [
            grad_key_h.transpose(1, 0, 2).reshape(seq_total, kv_width),
            grad_value_h.transpose(1, 0, 2).reshape(seq_total, kv_width),
        ],
        axis=1,
    )
    grad_kv, rim_back = sum_key_grads(
        grad_kv_terms.astype(low).reshape(CTX, tok_rows, 2 * kv_width), grad_ext[:8]
    )
    rim_back = jnp.where(ctx_here < CTX - 1, rim_back[:rim_rows], 0.0)
    grad_inner_pre = grad_ext[rim_rows:] + jnp.pad(rim_back, ((tok_rows - rim_rows, 0), (0, 0)))
    grad_key_rot = grad_kv[:, :kv_width].reshape(tok_rows, KV_HEADS, HEAD_DIM)
    grad_key_low = (
        (rotate_back(grad_key_rot, angle_cos, angle_sin) * key_scale)
        .reshape(tok_rows, kv_width)
        .astype(low)
    )
    grad_query = grad_query_h.transpose(1, 0, 2, 3).reshape(tok_rows, HEADS, HEAD_DIM)
    grad_query_low = (
        (rotate_back(grad_query, angle_cos, angle_sin) * HEAD_DIM ** (-0.5))
        .reshape(tok_rows, q_width)
        .astype(low)
    )
    grads_one = jnp.concatenate(
        [
            grad_query_low,
            grad_key_low,
            grad_kv[:, kv_width:].astype(low),
            grad_gate_z.astype(low),
            grad_inner_pre.astype(low),
            jnp.pad(grad_step_raw.astype(low), ((0, 0), (0, COLS - step_at - SSM_HEADS))),
        ],
        axis=1,
    )
    grad_normed_one = right_trans(grads_one, full_one)
    _, pull_one = jax.vjp(rms_scale, residual_in, gain_one_f)
    grad_in_norm, grad_gain_one = pull_one(grad_normed_one)
    input_grad = grad_middle + grad_in_norm

    acts = jnp.concatenate(
        [
            attn_low.reshape(tok_rows, FSDP, 64),
            mixer_low.reshape(tok_rows, FSDP, 192),
            hidden_low.reshape(tok_rows, FSDP, 256),
        ],
        axis=2,
    ).transpose(1, 0, 2)
    small_grads = jnp.concatenate(
        [
            grad_gain_one.reshape(FSDP, 128),
            grad_conv.reshape(CONV, FSDP, 224).transpose(1, 0, 2).reshape(FSDP, CONV * 224),
            grad_conv_bias.reshape(FSDP, 224),
            grad_step_bias.reshape(FSDP, 3),
            grad_decay.reshape(FSDP, 3),
            grad_skip.reshape(FSDP, 3),
            grad_mixer_gain.reshape(FSDP, 192),
            grad_gain_two.reshape(FSDP, 128),
            jnp.zeros((FSDP, 2048 - SMALL), jnp.float32),
        ],
        axis=1,
    ).reshape(FSDP, 16, 128)
    sum12, sum3 = sum_weight_grads(
        jnp.stack([normed_low, normed_two_low]),
        jnp.stack([grads_one, grads_two]),
        acts,
        jnp.stack([grad_attn_in, grad_mixer_in, grad_down_in]),
        small_grads,
    )
    one, two, three = (
        sum12[0].astype(jnp.float32),
        sum12[1].astype(jnp.float32),
        sum3.astype(jnp.float32),
    )
    tiny = two[0:16, PAD_AT:COLS].reshape(-1)
    return (
        layer_out.astype(low)[None],
        input_grad[None],
        tiny[0:128],
        one[:, :q_width],
        one[:, q_width : q_width + kv_width],
        one[:, q_width + kv_width : z_at],
        three[0:64],
        one[:, z_at:inner_at],
        one[:, inner_at:step_at],
        one[:, step_at : step_at + SSM_HEADS],
        tiny[128:1024].reshape(CONV, 224),
        tiny[1024:1248],
        tiny[1248:1251],
        tiny[1251:1254],
        tiny[1254:1257],
        tiny[1257:1449],
        three[64:256],
        tiny[1449:1577],
        two[:, :ff_width],
        two[:, ff_width : 2 * ff_width],
        three[256:512],
    )


def solution(mesh):
    in_specs = (
        P("fsdp", "ctx", None),
        P("fsdp", "ctx"),
        P("fsdp"),
        P("fsdp", None),
        P("fsdp", None),
        P("fsdp", None),
        P("fsdp", None),
        P("fsdp", None),
        P("fsdp", None),
        P("fsdp", None),
        P(None, "fsdp"),
        P("fsdp"),
        P("fsdp"),
        P("fsdp"),
        P("fsdp"),
        P("fsdp"),
        P("fsdp", None),
        P("fsdp"),
        P("fsdp", None),
        P("fsdp", None),
        P("fsdp", None),
        P("fsdp", "ctx", None),
    )
    out_specs = (
        P("fsdp", "ctx", None),
        P("fsdp", "ctx", None),
        P("fsdp"),
        P("fsdp", None),
        P("fsdp", None),
        P("fsdp", None),
        P("fsdp", None),
        P("fsdp", None),
        P("fsdp", None),
        P("fsdp", None),
        P(None, "fsdp"),
        P("fsdp"),
        P("fsdp"),
        P("fsdp"),
        P("fsdp"),
        P("fsdp"),
        P("fsdp", None),
        P("fsdp"),
        P("fsdp", None),
        P("fsdp", None),
        P("fsdp", None),
    )
    return jax.shard_map(local, mesh=mesh, in_specs=in_specs, out_specs=out_specs, check_vma=False)
```

time: 2040 us -> 637 us (0.31)
  waiting for transfers between devices: 1490 us -> 0 us
  Pallas kernels: 0 us -> 388 us
  blocking collectives: 278 us -> 0 us
  local copies, waits for them, and re-layouts: 37.8 us -> 98.4 us
  matrix products: 113 us -> 71.3 us
    reduce_scatter x10 -> x0, waiting for transfers between devices: 811 us -> none  [the longest x1 88 us: local(): lax.psum_scatter(grad_w_down.astype(jnp.bfloat16), 'fsdp', scatter_dimens...]
    pallas_call x0 -> x6, Pallas kernels: none -> 388 us  [call_kernel(): pl.pallas_call(body, name=name, out_shape=outs, in_specs=[pl.BlockSpec(me...]
    all_gather x11 -> x0, waiting for transfers between devices: 381 us -> none  [the longest x1 69.3 us: local(): lax.all_gather(w_gate, 'fsdp', axis=0, tiled=True)]
    all_gather x9 -> x0, blocking collectives: 228 us -> none  [the longest x1 43.2 us: local(): seg_all = lax.all_gather(segment_ids, 'ctx', axis=1, tiled=True)[0]]
    psum x2 -> x0, waiting for transfers between devices: 226 us -> none  [the longest x1 116 us: local(): lax.psum(shard_query.astype(jnp.bfloat16), 'ctx').astype(jnp.float32)]
    unnamed x29 -> x0, waiting for transfers between devices: 70.2 us -> none
    unnamed x2 -> x0, blocking collectives: 50.1 us -> none
    slice x1 -> x32, local copies, waits for them, and re-layouts: 0.01 us -> 31.9 us  [the longest x1 9.49 us: local(): full_two = all12[1].reshape(FSDP * 128, COLS)]
  transfers between devices with their start and end apart: 28 -> 0, of which waited for: 23 -> 0; matrix products, arithmetic and copies ran while one was open for 7% -> 0% of each run, Pallas kernels for 0% -> 0%
where the time goes in v1:
time: 637 us; the launch traced here: 631 us
  Pallas kernels  388 us (61%)
  local copies, waits for them, and re-layouts  98.4 us (15%)
  matrix products  71.3 us (11%)
  other arithmetic  69 us (11%)
    pallas_call x6, Pallas kernels, call_kernel(): pl.pallas_call(body, name=name, out_shape=outs, in_specs=[pl.BlockSpec(me...  388 us
    unnamed x262, local copies, waits for them, and re-layouts  22.1 us
    dot_general x5, matrix products, right_trans(): lax.dot_general(left_side, right_side, (((1,), (1,)), ((), ())), preferre...  16 us
    dot_general x3, matrix products, ssd_output(): result = jnp.einsum('tsh,shp->thp', mixing, values_ssm, precision=highest)  13.7 us

profile of v1, /device:TPU:1, one launch (start us, length us, event | category | flops | bytes accessed | tf_op | source)
XLA Modules:
  0.0 631.4 jit_solution(330340154741727350)
XLA Ops:
  8.6 117.6 %gather_weights.1 = (bf16[2,8,128,4224]{3,2,1,0:T(8,128)(2,1)}, bf16[8,512,1024]{2,1,0:T(8,128)(2,1)}) custom-call(bf16[2,128,4224]{2,1,0:T(8,128)(2,1)} %pad_maximum_fusion.in12, bf16[512,1024]{1,0:T(8,128)(2,1)} %pad_maximum_fusion.2.in3), custom_call_target="tpu_custom_call" | custom-call | tf_op jit(solution)/shard_map/gather_weights/pallas_call | solution.py:241
  127.9 9.5 %fusion.190 = (bf16[1,8,128,4224]{3,2,1,0:T(8,128)(2,1)}, bf16[1,8,128,4224]{3,2,1,0:T(8,128)(2,1)S(1)}) fusion(bf16[2,8,128,4224]{3,2,1,0:T(8,128)(2,1)} %get-tuple-element.124), kind=kLoop, calls=%fused_computation.329 | loop fusion | bytes 34603008 | tf_op jit(solution)/shard_map/slice | solution.py:791
  144.3 19.2 %gather_keys.1 = (bf16[16,128,256]{2,1,0:T(8,128)(2,1)}, f32[8,1792]{1,0:T(8,128)}, s32[16,8,128]{2,1,0:T(8,128)}) custom-call(bf16[128,256]{1,0:T(8,128)(2,1)} %pad_maximum_fusion.7.kv, f32[8,1792]{1,0:T(8,128)} %slice.345.rim, s32[8,128]{1,0:T(8,128)} %broadcast_in_dim.261.seg), custom_call_target="tpu_custom_call" | custom-call | tf_op jit(solution)/shard_map/gather_keys/pallas_call | solution.py:241
  170.1 4.0 fusion.95
  182.9 25.8 %scan_forward.1 = (bf16[16,96,128]{2,1,0:T(8,128)(2,1)}, f32[16,24,128]{2,1,0:T(8,128)}) custom-call(bf16[16,96,128]{2,1,0:T(8,128)(2,1)} %bitcast.440, f32[24,128]{1,0:T(8,128)} %broadcast_in_dim.272.decay), custom_call_target="tpu_custom_call" | custom-call | tf_op jit(solution)/shard_map/scan_forward/pallas_call | solution.py:241
  208.7 2.4 convolution_bitcast_fusion.3
  211.7 5.0 fusion.73
  230.1 11.5 %while.30 = (s32[]{:T(128)}, bf16[2,128,4,64]{1,3,2,0:T(8,128)(2,1)}, f32[2,4,128]{2,1,0:T(4,128)}, bf16[2,2048,64]{1,2,0:T(8,128)(2,1)}, bf16[2,2048,64]{1,2,0:...) while((s32[]{:T(128)}, ...), condition=%wide.region_4.5_spmd.clone.clone, body=%wide.region_1.4_spmd.clone.sunk.clone | while | flops 278658560 | bytes 16477817 | solution.py:840
  248.3 5.4 fusion.182
  254.3 2.7 multiply_convert_fusion.1
  259.3 3.5 multiply_reduce_fusion.12
  267.7 2.3 copy.221
  275.8 18.5 %scan_backward.1 = bf16[16,96,128]{2,1,0:T(8,128)(2,1)} custom-call(bf16[16,96,128]{2,1,0:T(8,128)(2,1)} %bitcast.443, f32[16,24,128]{2,1,0:T(8,128)} %get-tuple-element.135.decays), custom_call_target="tpu_custom_call" | custom-call | tf_op jit(solution)/shard_map/scan_backward/pallas_call | solution.py:241
  305.7 5.9 fusion.97
  318.8 2.6 reduce_window_sum.34
  321.4 2.6 reduce_window_sum.33
  336.8 2.8 fusion.76
  341.9 4.8 multiply_reduce_fusion.3
  354.7 18.3 %while.31 = (s32[]{:T(128)}, f32[2,128,4,64]{1,3,2,0:T(8,128)}, bf16[2,2048,64]{1,2,0:T(8,128)(2,1)}, bf16[2,2048,64]{1,2,0:T(8,128)(2,1)}, bf16[2,2048,64]{1,2,...) while((s32[]{:T(128)}, f32[2,128,4,64]{1,3,2,0:T(8,128)}, ...), condition=%wide.region_11.12_spmd.clone.clone, body=%wide.region_9.11_spmd.clone.sunk.clone | while | flops 681311744 | bytes 41574688 | solution.py:955
  377.7 2.4 pad_maximum_fusion.3.terms
  380.1 18.1 %sum_key_grads.1 = (f32[128,256]{1,0:T(8,128)}, f32[8,1792]{1,0:T(8,128)}) custom-call(bf16[16,128,256]{2,1,0:T(8,128)(2,1)} %pad_maximum_fusion.3.terms, f32[8,1792]{1,0:T(8,128)} %pad_add_fusion.4.rim), custom_call_target="tpu_custom_call" | custom-call | tf_op jit(solution)/shard_map/sum_key_grads/pallas_call | solution.py:241
  403.3 3.1 fusion.132
  407.2 6.8 %fusion.125 = (f32[1024]{0:T(1024)S(1)}, f32[128]{0:T(128)S(1)}, f32[128,1024]{1,0:T(8,128)S(1)}) fusion(bf16[1,128,1024]{2,1,0:T(8,128)(2,1)S(1)} %copy-done.24, f32[128]{0:T(128)S(1)} %copy-done.107, f32[1024]{0:T(1024)S(1)} %copy-done.74, bf16[128,4224]{1,0:T(8,128)(2,1)} %pad_dynamic-update-slice_fusion, bf16[1024,4224]{1,0:T(8,128)(2,1)} %bitcast.402), kind=kOutput, calls=%fused_computation.186 | convolution fusion | flops 1108212608 | bytes 10527744 | tf_op jit(solution)/shard_map/dot_general | solution.py:33
  424.5 188.8 %sum_weight_grads.1 = (bf16[2,128,4224]{2,1,0:T(8,128)(2,1)}, bf16[512,1024]{1,0:T(8,128)(2,1)}) custom-call(bf16[2,128,1024]{2,1,0:T(8,128)(2,1)} %pad_maximum_fusion.6.norms, bf16[2,128,4224]{2,1,0:T(8,128)(2,1)} %pad_maximum_fusion.1.grads12, bf16[8,128,512]{2,1,0:T(8,128)(2,1)} %maximum_bitcast_fusion.acts, ...), custom_call_target="tpu_custom_call" | custom-call | tf_op jit(solution)/shard_map/sum_weight_grads/pallas_call | solution.py:241
  (504 shorter events, 173.1 us)
Async XLA Ops:
  8.6 119.1 %copy-start.22 = (bf16[1,128,1024]{2,1,0:T(8,128)(2,1)S(1)}, bf16[1,128,1024]{2,1,0:T(8,128)(2,1)}, u32[]{:S(2)}) copy-start(bf16[1,128,1024]{2,1,0:T(8,128)(2,1)} %param.26) | copy-start | bytes 786436
  127.0 92.9 %copy-start.57 = (f32[1,8,16,128]{3,1,2,0:T(8,128)}, f32[1,8,16,128]{3,1,2,0:T(8,128)S(1)}, u32[]{:S(2)}) copy-start(f32[1,8,16,128]{3,1,2,0:T(8,128)S(1)} %copy.263) | copy-start | bytes 196612
  127.6 9.8 %copy-start.73 = (f32[1024]{0:T(1024)}, f32[1024]{0:T(1024)S(1)}, u32[]{:S(2)}) copy-start(f32[1024]{0:T(1024)S(1)} %get-tuple-element.410) | copy-start | bytes 12292
  127.8 9.7 %copy-start.113 = (f32[128]{0:T(128)}, f32[128]{0:T(128)S(1)}, u32[]{:S(2)}) copy-start(f32[128]{0:T(128)S(1)} %fusion.122) | copy-start | bytes 1540
  127.8 9.7 %copy-start.106 = (f32[128]{0:T(128)}, f32[128]{0:T(128)S(1)}, u32[]{:S(2)}) copy-start(f32[128]{0:T(128)S(1)} %fusion.169) | copy-start | bytes 1540
  127.9 9.5 %copy-start.33 = (bf16[1,128,1024]{2,1,0:T(8,128)(2,1)}, bf16[1,128,1024]{2,1,0:T(8,128)(2,1)S(1)}, u32[]{:S(2)}) copy-start(bf16[1,128,1024]{2,1,0:T(8,128)(2,1)S(1)} %fusion.127) | copy-start | bytes 786436
  167.4 44.1 %copy-start.39 = (f32[128,24]{1,0:T(8,128)}, f32[128,24]{1,0:T(8,128)S(1)}, u32[]{:S(2)}) copy-start(f32[128,24]{1,0:T(8,128)S(1)} %get-tuple-element.370) | copy-start | bytes 36868
  167.7 9.8 %copy-start.78 = (f32[128,24]{0,1:T(8,128)}, f32[128,24]{0,1:T(8,128)S(1)}, u32[]{:S(2)}) copy-start(f32[128,24]{0,1:T(8,128)S(1)} %copy.214) | copy-start | bytes 36868
  174.2 36.9 %copy-start.5 = (f32[128,1792]{1,0:T(8,128)}, f32[128,1792]{1,0:T(8,128)S(1)}, u32[]{:S(2)}) copy-start(f32[128,1792]{1,0:T(8,128)S(1)} %get-tuple-element.371) | copy-start | bytes 2752516
  248.2 14.6 %copy-start.3 = (f32[128,1024]{1,0:T(8,128)}, f32[128,1024]{1,0:T(8,128)S(1)}, u32[]{:S(2)}) copy-start(f32[128,1024]{1,0:T(8,128)S(1)} %get-tuple-element.427) | copy-start | bytes 1572868
  273.1 21.2 %copy-start.30 = (bf16[16,96,128]{2,1,0:T(8,128)(2,1)S(1)}, bf16[16,96,128]{2,1,0:T(8,128)(2,1)}, u32[]{:S(2)}) copy-start(bf16[16,96,128]{2,1,0:T(8,128)(2,1)} %get-tuple-element.130) | copy-start | bytes 1179652
  328.3 8.5 %copy-start.36 = (f32[128,1536]{0,1:S(1)}, f32[128,1536]{0,1}, u32[]{:S(2)}) copy-start(f32[128,1536]{0,1} %copy-done.35) | copy-start | bytes 2359300
  328.3 8.5 %copy-start.37 = (f32[128,1536]{0,1:T(8,128)S(1)}, f32[128,1536]{0,1:T(8,128)}, u32[]{:S(2)}) copy-start(f32[128,1536]{0,1:T(8,128)} %copy.221) | copy-start | bytes 2359300
  328.3 8.5 %copy-start.76 = (f32[128,128]{1,0:T(8,128)S(1)}, f32[128,128]{1,0:T(8,128)}, u32[]{:S(2)}) copy-start(f32[128,128]{1,0:T(8,128)} %copy-done.75) | copy-start | bytes 196612
  328.3 8.4 %copy-start.79 = (f32[128,24]{0,1:T(8,128)S(1)}, f32[128,24]{0,1:T(8,128)}, u32[]{:S(2)}) copy-start(f32[128,24]{0,1:T(8,128)} %copy-done.78) | copy-start | bytes 36868
  328.4 8.4 %copy-start.88 = (pred[128,128]{1,0:T(8,128)(4,1)S(1)}, pred[128,128]{1,0:T(8,128)(4,1)}, u32[]{:S(2)}) copy-start(pred[128,128]{1,0:T(8,128)(4,1)} %copy-done.87) | copy-start | bytes 49156
  328.4 8.4 %copy-start.91 = (f32[128,24]{0,1:T(8,128)S(1)}, f32[128,24]{0,1:T(8,128)}, u32[]{:S(2)}) copy-start(f32[128,24]{0,1:T(8,128)} %copy-done.90) | copy-start | bytes 36868
  376.5 22.7 %copy-start.53 = (f32[128,32]{0,1:T(8,128)S(1)}, f32[128,32]{0,1:T(8,128)}, u32[]{:S(2)}) copy-start(f32[128,32]{0,1:T(8,128)} %copy-done.52) | copy-start | bytes 49156
  376.5 22.7 %copy-start.55 = (f32[128,32]{0,1:T(8,128)S(1)}, f32[128,32]{0,1:T(8,128)}, u32[]{:S(2)}) copy-start(f32[128,32]{0,1:T(8,128)} %copy-done.54) | copy-start | bytes 49156
  377.7 21.6 %copy-start.60 = (f32[2,128,4,64]{1,3,2,0:T(8,128)S(1)}, f32[2,128,4,64]{1,3,2,0:T(8,128)}, u32[]{:S(2)}) copy-start(f32[2,128,4,64]{1,3,2,0:T(8,128)} %get-tuple-element.132) | copy-start | bytes 786436
  380.1 20.3 %copy-start.96 = (f32[128]{0:T(128)S(1)}, f32[128]{0:T(128)}, u32[]{:S(2)}) copy-start(f32[128]{0:T(128)} %copy-done.94) | copy-start | bytes 1540
  380.1 20.4 %copy-start.110 = (f32[128]{0:T(128)S(1)}, f32[128]{0:T(128)}, u32[]{:S(2)}) copy-start(f32[128]{0:T(128)} %copy-done.109) | copy-start | bytes 1540
  617.2 9.6 %copy-start.29 = (bf16[512,1024]{1,0:T(8,128)(2,1)S(1)}, bf16[512,1024]{1,0:T(8,128)(2,1)}, u32[]{:S(2)}) copy-start(bf16[512,1024]{1,0:T(8,128)(2,1)} %get-tuple-element.139) | copy-start | bytes 3145732
  619.1 10.4 %copy-start.4 = (f32[128,1024]{1,0:T(8,128)S(1)}, f32[128,1024]{1,0:T(8,128)}, u32[]{:S(2)}) copy-start(f32[128,1024]{1,0:T(8,128)} %copy-done.3) | copy-start | bytes 1572868
  (114 other events, 440.6 us)
